TPU v7x, 128 devices: a whole 4x4x4 slice. The times are simulated.
128 devices in a mesh: face: 8 (over y, core), tile: 16 (over z, x).
Axes of the slice: x: 4, y: 4, z: 4, core: 2. Of those that a mesh axis runs over, the one named last changes fastest.
Arguments:
- atm_tangent: float32 [64, 1048576], P(None, ('face', 'tile')), may hold values from -6 to 6
- atm_mixing: bfloat16 [63, 1048576], P(None, ('face', 'tile')), may hold values from 0.049804688 to 0.23925781
- flux_coef: float32 [4, 64], replicated, may hold values from -0.75 to 0.75
- remap_weight: bfloat16 [32768, 128, 128], P(('face', 'tile')), may hold values from -0.5 to 0.5
- target_device: int32 [8192, 4], P(('face', 'tile')), may hold values from 0 to 127, all different within a row; in each aligned block of 64 rows (0 to 63, 64 to 127, ...) at most 4 rows name the same one
- target_row: int32 [8192, 4], P(('face', 'tile')), may hold values from 0 to 63
- ocean_tangent: float32 [75, 512, 2048], P(None, 'face', 'tile'), may hold values from -6 to 6
- ocean_mixing: float32 [74], replicated, may hold values from 0.02 to 0.2
- penetration: float32 [75, 4], replicated, may hold values from -0.75 to 0.75
- sea_mask: int32 [512, 2048], P('face', 'tile'), may hold values 0 or 1
- ocean_adjoint: float32 [75, 512, 2048], P(None, 'face', 'tile'), may hold values from -6 to 6
Outputs:
- ocean_forward: float32 [75, 512, 2048], P(None, 'face', 'tile')
- ocean_backward: float32 [75, 512, 2048], P(None, 'face', 'tile')
- atm_adjoint: float32 [64, 1048576], P(None, ('face', 'tile'))
Inputs may be any that keep to these rules, and one draw needn't show every extreme that they name: `target_device`: among one device's intersections no device is named more than 4 times; in every draw some device's intersections name one device exactly 4 times; the 4 devices of one block differ.
All inputs are finite; a program needn't handle non-finite values. No bound on the sum of `sea_mask` on one device may be relied on, other than what follows from the above.
Results may differ from a plain program's by a relative error of at most 0.0003.
Values sent between devices are 32-bit elements; how exact they have to be, the bound alone decides.
No kernel may reach another device: no remote copies, remote signals or barrier semaphores. Data moves between devices by JAX's collectives and lax.ppermute only.
A program may use at most 128 MiB of HBM per device.

v0:
```python
import functools

import jax
import jax.numpy as jnp
from jax import lax
from jax.experimental import pallas as pl
from jax.experimental.pallas import tpu as pltpu
from jax.sharding import PartitionSpec as P

ATM_SWEEPS = 4
HRATE = 0.1
LA = 64
LO = 75
FLD = 4
B = 128
NBA = 64
KO = 4
OY = 64
CAP = 4
DEV = 128
MSG = CAP * FLD + 1
GRP = 8
STEPS = NBA // GRP
PLANES = 3
ROWS = 72
TOP = 16
TALL = 96
LEVELS = 25
F32 = jnp.float32
BF16 = jnp.bfloat16
MIB = 1024 * 1024
SMEM = pl.BlockSpec(memory_space=pltpu.SMEM)
VMEM = pl.BlockSpec(memory_space=pltpu.VMEM)
ANY = pl.BlockSpec(memory_space=pl.ANY)
PITCH = LA + 1
ALONE = 58


def params(mib):
    return pltpu.CompilerParams(vmem_limit_bytes=mib * MIB)


def f32(*shape):
    return jax.ShapeDtypeStruct(shape, F32)


def split2(v):
    hi = v.astype(BF16)
    return hi, (v - hi.astype(F32)).astype(BF16)


def dot(a, b, dims=((1,), (0,))):
    return lax.dot_general(a, b, (dims, ((), ())), preferred_element_type=F32)


def lanes(rows):
    return lax.broadcasted_iota(jnp.int32, (rows, B), 1)


def sweep_levels(load, mixing, emit):
    values = [{} for _ in range(ATM_SWEEPS + 1)]
    flows = [{} for _ in range(ATM_SWEEPS)]
    mix = {}
    for t in range(LA + ATM_SWEEPS):
        if t < LA:
            values[0][t] = load(t)
            if t < LA - 1:
                mix[t] = mixing(t)
        for s in range(ATM_SWEEPS):
            l = t - 1 - s
            if not 0 <= l < LA:
                continue
            v = values[s][l]
            done = v
            if l < LA - 1:
                flows[s][l] = mix[l] * (values[s][l + 1] - v)
                done = done + flows[s][l]
            if l > 0:
                done = done - flows[s][l - 1]
            values[s + 1][l] = done
            if s == ATM_SWEEPS - 1:
                emit(l, done)


def level_rows(ref, level):
    return ref[pl.ds(level, GRP, stride=PITCH), :]


def block_lanes(block):
    return pl.ds(pl.multiple_of(block * B, B), B)


def square(w_ref, block, k):
    at = block * KO + k
    return jnp.concatenate(
        [
            jnp.concatenate([w_ref[at], w_ref[at + 1]], axis=1),
            jnp.concatenate([w_ref[at + KO], w_ref[at + KO + 1]], axis=1),
        ],
        axis=0,
    )


def surface_flux_kernel(coef_ref, x_ref, mix_ref, out_ref, xs, ms):
    def work(step, carry):
        for b in range(GRP):
            at = block_lanes(step * GRP + b)
            xs[step % 2, pl.ds(b * PITCH, LA), :] = x_ref[:, at]
            ms[step % 2, pl.ds(b * PITCH, LA - 1), :] = mix_ref[:, at].astype(F32)
        sums = [None] * FLD

        def emit(level, v):
            for f in range(FLD):
                term = coef_ref[f, level] * v
                sums[f] = term if sums[f] is None else sums[f] + term

        sweep_levels(
            lambda l: level_rows(xs.at[step % 2], l), lambda l: level_rows(ms.at[step % 2], l), emit
        )
        for f in range(FLD):
            high = sums[f].astype(BF16).astype(F32)
            at = step * GRP * 2 * FLD + f
            out_ref[pl.ds(at, GRP, stride=2 * FLD), :] = high
            out_ref[pl.ds(at + FLD, GRP, stride=2 * FLD), :] = sums[f] - high
        return carry

    lax.fori_loop(0, STEPS, work, 0, unroll=2)


def surface_flux(coef, x, mix):
    return pl.pallas_call(
        surface_flux_kernel,
        in_specs=[SMEM, VMEM, VMEM],
        out_specs=VMEM,
        out_shape=f32(NBA * 2 * FLD, B),
        scratch_shapes=[pltpu.VMEM((2, GRP * PITCH, B), F32), pltpu.VMEM((2, GRP * PITCH, B), F32)],
        compiler_params=params(12),
        name="surface_flux",
    )(coef, x, mix)


def remap_kernel(td_ref, tr_ref, pair_ref, w_ref, out_ref, slot_ref, count):
    out_ref[...] = jnp.zeros_like(out_ref)

    def clear(d, c):
        count[d] = 0
        return c

    lax.fori_loop(0, DEV, clear, 0, unroll=8)
    lane = lanes(1)
    upper = lax.broadcasted_iota(jnp.int32, (4 * FLD, B), 0) < 2 * FLD

    def work(step, carry):
        for i in range(0, GRP, 2):
            row = step * GRP + i
            both = pair_ref[pl.ds(pl.multiple_of(row * 2 * FLD, 4 * FLD), 4 * FLD), :]
            lhs = jnp.concatenate(
                [jnp.where(upper, both, 0.0), jnp.where(upper, 0.0, both)], axis=1
            ).astype(BF16)
            for k in range(0, KO, 2):
                moved = dot(lhs, square(w_ref, row, k))
                for a in range(2):
                    total = moved[8 * a : 8 * a + 4] + moved[8 * a + 4 : 8 * a + 8]
                    for b in range(2):
                        dev = td_ref[k + b, row + a]
                        place = count[dev]
                        count[dev] = place + 1
                        slot_ref[(row + a) * KO + k + b] = dev * CAP + place
                        at = dev * MSG
                        out_ref[pl.ds(at + place * FLD, FLD), :] = total[:, b * B : (b + 1) * B]
                        label = (tr_ref[k + b, row + a] + 1).astype(F32)
                        last = pl.ds(at + MSG - 1, 1)
                        out_ref[last, :] = jnp.where(lane == place, label, out_ref[last, :])
        return carry

    lax.fori_loop(0, STEPS, work, 0, unroll=STEPS)


def remap(td, tr, pair, w):
    return pl.pallas_call(
        remap_kernel,
        in_specs=[SMEM, SMEM, VMEM, VMEM],
        out_specs=[VMEM, SMEM],
        out_shape=[f32(DEV * MSG, B), jax.ShapeDtypeStruct((NBA * KO,), jnp.int32)],
        scratch_shapes=[pltpu.SMEM((DEV,), jnp.int32)],
        compiler_params=params(16),
        name="remap",
    )(td, tr, pair, w)


def atm_adjoint_kernel(
    slot_ref, coef_ref, back_ref, mix_ref, w_hbm, out_hbm, w_ref, ms, total_ref, steps_ref, out_ref, sems
):
    cols = GRP * B

    def w_copy(s):
        part = pl.ds(s * GRP * KO, GRP * KO)
        return pltpu.make_async_copy(w_hbm.at[part], w_ref.at[part], sems.at[0, s])

    def out_copy(s):
        part = pl.ds(pl.multiple_of(s * cols, cols), cols)
        return pltpu.make_async_copy(out_ref.at[:, part], out_hbm.at[:, part], sems.at[1, s])

    for s in range(STEPS):
        w_copy(s).start()

    def work(step, carry):
        w_copy(step).wait()
        for i in range(0, GRP, 2):
            row = step * GRP + i
            total = None
            for k in range(0, KO, 2):
                blocks = []
                for a in range(2):
                    pieces = []
                    for b in range(2):
                        v = back_ref[slot_ref[(row + a) * KO + k + b]]
                        high = v.astype(BF16).astype(F32)
                        pieces.append(jnp.concatenate([high, v - high], axis=0))
                    blocks.append(jnp.concatenate(pieces, axis=1))
                lhs = jnp.concatenate(blocks, axis=0).astype(BF16)
                part = dot(lhs, square(w_ref, row, k), ((1,), (1,)))
                total = part if total is None else total + part
            total_ref[pl.ds(i * FLD, FLD), :] = total[0:4, 0:B] + total[4:8, 0:B]
            total_ref[pl.ds((i + 1) * FLD, FLD), :] = total[8:12, B:] + total[12:16, B:]
        for b in range(GRP):
            ms[pl.ds(b * PITCH, LA - 1), :] = mix_ref[:, block_lanes(step * GRP + b)].astype(F32)
        fields = [total_ref[pl.ds(f, GRP, stride=FLD), :] for f in range(FLD)]

        def load(level):
            v = coef_ref[0, level] * fields[0]
            for f in range(1, FLD):
                v = v + coef_ref[f, level] * fields[f]
            return v

        def emit(level, v):
            steps_ref[pl.ds(level, GRP, stride=PITCH), :] = v

        sweep_levels(load, lambda l: level_rows(ms, l), emit)
        for b in range(GRP):
            out_ref[:, block_lanes(step * GRP + b)] = steps_ref[pl.ds(b * PITCH, LA), :]
        out_copy(step).start()
        return carry

    lax.fori_loop(0, STEPS, work, 0, unroll=2)
    for s in range(STEPS):
        out_copy(s).wait()


def atm_adjoint(slots, coef, back, mix, w):
    return pl.pallas_call(
        atm_adjoint_kernel,
        in_specs=[SMEM, SMEM, VMEM, VMEM, ANY],
        out_specs=ANY,
        out_shape=f32(LA, NBA * B),
        scratch_shapes=[
            pltpu.VMEM((NBA * KO, B, B), BF16),
            pltpu.VMEM((GRP * PITCH, B), F32),
            pltpu.VMEM((GRP * FLD, B), F32),
            pltpu.VMEM((GRP * PITCH, B), F32),
            pltpu.VMEM((LA, NBA * B), F32),
            pltpu.SemaphoreType.DMA((2, STEPS)),
        ],
        compiler_params=params(ALONE),
        name="atm_adjoint",
    )(slots, coef, back, mix, w)


def rows_kernel(a_hbm, t_hbm, m_hbm, low_ref, high_ref, a_ref, t_ref, m_ref, sems):
    copies = []
    for i, r in enumerate((0, OY - 8)):
        rows = pl.ds(r, 8)
        copies += [
            pltpu.make_async_copy(a_hbm.at[:, rows], a_ref.at[i], sems.at[0, i]),
            pltpu.make_async_copy(t_hbm.at[:, rows], t_ref.at[i], sems.at[1, i]),
            pltpu.make_async_copy(m_hbm.at[rows], m_ref.at[i], sems.at[2, i]),
        ]
    for c in copies:
        c.start()
    for c in copies:
        c.wait()
    low_ref[0:LO] = a_ref[0, :, 0:2, :] * m_ref[0, 0:2].astype(F32)
    low_ref[LO:] = t_ref[0, :, 0:2, :]
    high_ref[0:LO] = a_ref[1, :, 6:8, :] * m_ref[1, 6:8].astype(F32)
    high_ref[LO:] = t_ref[1, :, 6:8, :]


def edge_rows(adjoint, tangent, mask):
    return pl.pallas_call(
        rows_kernel,
        in_specs=[ANY] * 3,
        out_specs=[VMEM, VMEM],
        out_shape=[f32(2 * LO, 2, B), f32(2 * LO, 2, B)],
        scratch_shapes=[
            pltpu.VMEM((2, LO, 8, B), F32),
            pltpu.VMEM((2, LO, 8, B), F32),
            pltpu.VMEM((2, 8, B), jnp.int32),
            pltpu.SemaphoreType.DMA((3, 2)),
        ],
        compiler_params=params(ALONE),
        name="edge_rows",
    )(adjoint, tangent, mask)


def level_lanes(plane):
    return range(min(32, LO - 32 * plane))


def pack_kernel(a_ref, t_ref, mask_ref, north_ref, south_ref, own_ref, east_ref, west_ref):
    sea = mask_ref[...].astype(F32)
    lane = lanes(1)
    part = lane % 4
    for plane in range(PLANES):
        held = []
        for at, x_ref in ((0, a_ref), (LO, t_ref)):
            body = jnp.zeros((OY, B), F32)
            rim = jnp.zeros((2, B), F32)
            for m in level_lanes(plane):
                level = 32 * plane + m
                mine = lane // 4 == m
                body = jnp.where(mine, pltpu.roll(x_ref[level], (4 * m + 2) % B, 1), body)
                edge = jnp.concatenate(
                    [south_ref[at + level, 0:1], north_ref[at + level, 1:2]], axis=0
                )
                rim = jnp.where(mine, pltpu.roll(edge, (4 * m + 2) % B, 1), rim)
            if at == 0:
                body = body * jnp.where(part < 2, edge_mask(sea, part, True), edge_mask(sea, part, False))
            held.append(
                jnp.concatenate([body, rim[0:1], jnp.zeros((6, B), F32), rim[1:2]], axis=0)
            )
        adj, tan = held
        own_ref[0, plane] = adj
        own_ref[1, plane] = tan
        east_ref[plane] = jnp.where(part < 2, adj, pltpu.roll(tan, 2, 1))
        west_ref[plane] = jnp.where(part < 2, pltpu.roll(adj, B - 2, 1), tan)


def edge_mask(sea, part, high):
    first = B - 2 if high else 0
    return jnp.where(part % 2 == 0, sea[:, first : first + 1], sea[:, first + 1 : first + 2])


def pack_columns(adjoint, tangent, mask, north, south):
    return pl.pallas_call(
        pack_kernel,
        out_shape=[f32(2, PLANES, ROWS, B), f32(PLANES, ROWS, B), f32(PLANES, ROWS, B)],
        compiler_params=params(12),
        name="pack_columns",
    )(adjoint, tangent, mask, north, south)


def lateral_table():
    r = lax.broadcasted_iota(jnp.int32, (B, B), 0)
    c = lax.broadcasted_iota(jnp.int32, (B, B), 1)
    near = ((r - c == 1) | (c - r == 1)).astype(F32).astype(BF16)
    return jnp.concatenate([near, near], axis=0)


def swapped(v, part):
    return jnp.where(part == 2, pltpu.roll(v, 1, 1), pltpu.roll(v, B - 1, 1))


def around_rows(v):
    return pltpu.roll(v, 1, 0) + pltpu.roll(v, ROWS - 1, 0)


def ocean_kernel(adjoint, k_ref, ends_ref, pen_ref, x_ref, mask_ref, north_ref, south_ref,
                 own_ref, west_ref, east_ref, *rest):
    if adjoint:
        out_hbm, flux_ref, state, first, fix, out_ref, sem = rest
    else:
        out_hbm, state, first, fix, out_ref, sem = rest
    sea = mask_ref[...].astype(F32)

    state[:, 8:TOP, :] = jnp.zeros((LO + 1, 8, B), F32)
    state[:, TOP + OY : TOP + OY + 8, :] = jnp.zeros((LO + 1, 8, B), F32)
    state[0:LO, TOP - 2 : TOP, :] = north_ref[...]
    state[0:LO, TOP + OY : TOP + OY + 2, :] = south_ref[...]
    state[LO, TOP : TOP + OY] = jnp.zeros((OY, B), F32)

    def fill(level, carry):
        v = x_ref[level]
        state[level, TOP : TOP + OY] = v * sea if adjoint else v
        return carry

    lax.fori_loop(0, LO, fill, 0, unroll=5)

    lane = lanes(1)
    part = lane % 4
    ups, downs = [], []
    for plane in range(PLANES):
        up = jnp.zeros((1, B), F32)
        down = jnp.zeros((1, B), F32)
        for m in level_lanes(plane):
            level = 32 * plane + m
            mine = lane // 4 == m
            if level < LO - 1:
                up = jnp.where(mine, k_ref[level], up)
            if level > 0:
                down = jnp.where(mine, k_ref[level - 1], down)
        ups.append(up)
        downs.append(down)
    own = [own_ref[0, p] for p in range(PLANES)]
    if adjoint:
        outer = [
            jnp.where(part < 2, west_ref[p], pltpu.roll(east_ref[p], 2, 1)) for p in range(PLANES)
        ]
    else:
        outer = [
            jnp.where(part < 2, pltpu.roll(west_ref[p], B - 2, 1), east_ref[p])
            for p in range(PLANES)
        ]

    def vertical(vs, p):
        c = vs[p]
        higher = pltpu.roll(c, B - 4, 1)
        if p + 1 < PLANES:
            higher = jnp.where(lane < B - 4, higher, pltpu.roll(vs[p + 1], B - 4, 1))
        lower = pltpu.roll(c, 4, 1)
        if p > 0:
            lower = jnp.where(lane >= 4, lower, pltpu.roll(vs[p - 1], 4, 1))
        return c + ups[p] * (higher - c) - downs[p] * (c - lower)

    inner = (part == 1) | (part == 2)
    added = [jnp.where(inner, HRATE * swapped(c, part), 0.0) for c in outer]
    for p in range(PLANES):
        c = outer[p]
        from_west = jnp.where(part == 1, pltpu.roll(c, 1, 1), pltpu.roll(own[p], 1, 1))
        from_east = jnp.where(part == 1, pltpu.roll(own[p], B - 1, 1), pltpu.roll(c, B - 1, 1))
        beyond = vertical(outer, p) + HRATE * (from_west + from_east + around_rows(c) - 4.0 * c)
        e = added[p]
        side = HRATE * (pltpu.roll(e, B - 1, 1) + pltpu.roll(e, 1, 1))
        here = vertical(added, p) + HRATE * (around_rows(e) - 4.0 * e + swapped(beyond, part))
        fix[p] = jnp.where(inner, here, side)[0:OY]

    table = lateral_table()
    first[LO] = jnp.zeros((TALL, B), F32)
    row = lax.broadcasted_iota(jnp.int32, (OY + 16, B), 0) + 8
    keep = jnp.where(
        row == TOP - 1, ends_ref[0].astype(F32), jnp.where(row == TOP + OY, ends_ref[1].astype(F32), 1.0)
    )
    wide = lanes(OY)
    edge_lane = (wide < 2) | (wide >= B - 2)

    def step(src, start, count, second):
        rows = pl.ds(start, count)

        def body(group, below):
            base = group * LEVELS
            vs = [src[base + j, rows, :] for j in range(LEVELS + 1)]
            hi, lo = split2(jnp.concatenate(vs[:LEVELS], axis=0))
            side = dot(jnp.concatenate([hi, lo], axis=1), table)
            for j in range(LEVELS):
                level = base + j
                v = vs[j]
                k = jnp.where(level < LO - 1, k_ref[jnp.minimum(level, LO - 2)], 0.0)
                flow = k * (vs[j + 1] - v)
                near = (
                    src[level, pl.ds(start - 1, count), :]
                    + src[level, pl.ds(start + 1, count), :]
                    + side[j * count : (j + 1) * count]
                )
                done = v * (1.0 - 4.0 * HRATE) + (flow - below) + HRATE * near
                if second:
                    shift = (2 * B - 2 - 4 * (level % 32)) % B
                    extra = pltpu.roll(fix[level // 32], shift, 1)
                    done = done + jnp.where(edge_lane, extra, 0.0)
                    out_ref[level] = done
                else:
                    first[level, rows, :] = done * keep
                below = flow
            return below

        lax.fori_loop(0, LO // LEVELS, body, jnp.zeros((count, B), F32))

    step(state, 8, OY + 16, False)
    step(first, TOP, OY, True)
    out_copy = pltpu.make_async_copy(out_ref, out_hbm, sem.at[0])
    out_copy.start()

    if adjoint:
        tall = 32
        for r in range(0, OY, tall):
            rows = pl.ds(r, tall)

            def project(level, sums):
                v = out_ref[level, rows, :]
                return tuple(s + pen_ref[f, level] * v for f, s in enumerate(sums))

            sums = lax.fori_loop(
                0, LO, project, tuple(jnp.zeros((tall, B), F32) for _ in range(FLD)), unroll=5
            )
            for f in range(FLD):
                flux_ref[rows, f * B : (f + 1) * B] = sums[f]
    out_copy.wait()


def ocean_steps(adjoint, k, ends, pen, x, mask, north, south, own, west, east):
    at = 0 if adjoint else 1
    rim = pl.BlockSpec((LO, 2, B), lambda i: (at, 0, 0))
    full = lambda *shape: pl.BlockSpec(shape, lambda i: (0,) * len(shape))
    shapes = [f32(LO, OY, B)]
    outs = [ANY]
    if adjoint:
        shapes.append(f32(OY, FLD * B))
        outs.append(full(OY, FLD * B))
    return pl.pallas_call(
        functools.partial(ocean_kernel, adjoint),
        grid=(1,),
        in_specs=[
            SMEM,
            SMEM,
            SMEM,
            full(LO, OY, B),
            full(OY, B),
            rim,
            rim,
            pl.BlockSpec((1, PLANES, ROWS, B), lambda i: (at, 0, 0, 0)),
            full(PLANES, ROWS, B),
            full(PLANES, ROWS, B),
        ],
        out_specs=outs,
        out_shape=shapes,
        scratch_shapes=[
            pltpu.VMEM((LO + 1, TALL, B), F32),
            pltpu.VMEM((LO + 1, TALL, B), F32),
            pltpu.VMEM((PLANES, OY, B), F32),
            pltpu.VMEM((LO, OY, B), F32),
            pltpu.SemaphoreType.DMA((1,)),
        ],
        compiler_params=params(24),
        name="ocean_adjoint" if adjoint else "ocean_tangent",
    )(k, ends, pen, x, mask, north, south, own, west, east)


def answer_kernel(msg_ref, flux_ref, out_ref):
    labels = msg_ref[pl.ds(MSG - 1, DEV, stride=MSG), :]
    gh, gl = split2(flux_ref[...])
    table = jnp.concatenate([gh, gl], axis=0)
    want = lax.broadcasted_iota(jnp.int32, (DEV, B), 1) % OY + 1
    for c in range(CAP):
        pick = (labels[:, c : c + 1].astype(jnp.int32) == want).astype(F32).astype(BF16)
        rows = dot(pick, table)
        for f in range(FLD):
            out_ref[pl.ds(c * FLD + f, DEV, stride=CAP * FLD), :] = rows[:, f * B : (f + 1) * B]


def answer(msg, flux):
    return pl.pallas_call(
        answer_kernel,
        out_shape=f32(DEV * CAP * FLD, B),
        compiler_params=params(12),
        name="answer",
    )(msg, flux)


def collect_kernel(msg_ref, flux_ref, low_ref, high_ref):
    labels = msg_ref[pl.ds(MSG - 1, DEV, stride=MSG), :].T.astype(jnp.int32)
    rows = lax.broadcasted_iota(jnp.int32, (OY, DEV), 0) + 1
    total = jnp.zeros((OY, FLD * B), F32)
    for c in range(CAP):
        pick = (labels[c : c + 1, :] == rows).astype(F32).astype(BF16)
        data = jnp.concatenate(
            [msg_ref[pl.ds(c * FLD + f, DEV, stride=MSG), :] for f in range(FLD)], axis=1
        )
        dh, dl = split2(data)
        total = total + dot(jnp.concatenate([pick, pick], axis=1), jnp.concatenate([dh, dl], axis=0))
    for f in range(FLD):
        v = total[:, f * B : (f + 1) * B]
        flux_ref[f] = v
        low_ref[f] = v[0:2]
        high_ref[f] = v[OY - 2 : OY]


def collect(msg):
    return pl.pallas_call(
        collect_kernel,
        out_shape=[f32(FLD, OY, B), f32(FLD, 2, B), f32(FLD, 2, B)],
        compiler_params=params(12),
        name="collect",
    )(msg)


def circular(flux_ref, north_ref, south_ref, f):
    return jnp.concatenate(
        [flux_ref[f], south_ref[f], jnp.zeros((ROWS - OY - 4, B), F32), north_ref[f]], axis=0
    )


def flux_columns_kernel(flux_ref, north_ref, south_ref, own_ref, out_ref):
    lane = lanes(1)
    held = jnp.zeros((ROWS, B), F32)
    for f in range(FLD):
        v = circular(flux_ref, north_ref, south_ref, f)
        held = jnp.where(lane // 4 == f, pltpu.roll(v, 4 * f + 2, 1), held)
    own_ref[...] = held
    square = jnp.concatenate([held, jnp.zeros((B - ROWS, B), F32)], axis=0)
    out_ref[...] = square.T[0 : 4 * FLD]


def flux_columns(flux, north, south):
    return pl.pallas_call(
        flux_columns_kernel,
        out_shape=[f32(ROWS, B), f32(4 * FLD, B)],
        compiler_params=params(12),
        name="flux_columns",
    )(flux, north, south)


def unsent(ref):
    return jnp.concatenate([ref[...], jnp.zeros((B - 4 * FLD, B), F32)], axis=0).T[0:ROWS]


def apply_flux_kernel(
    coef_ref, ends_ref, x_ref, mask_ref, flux_ref, north_ref, south_ref, own_ref, west_ref, east_ref,
    out_hbm, terms, out_ref, sems
):
    lane = lanes(1)
    part = lane % 4
    own = own_ref[...]
    outer = jnp.where(part < 2, unsent(west_ref), unsent(east_ref))
    from_west = jnp.where(part == 1, pltpu.roll(outer, 1, 1), pltpu.roll(own, 1, 1))
    from_east = jnp.where(part == 1, pltpu.roll(own, B - 1, 1), pltpu.roll(outer, B - 1, 1))
    beyond = from_west + from_east + around_rows(outer) - 4.0 * outer
    outer, beyond = swapped(outer, part), swapped(beyond, part)
    ring = lax.broadcasted_iota(jnp.int32, (ROWS, B), 0)
    keep = jnp.where(
        ring == ROWS - 1, ends_ref[0].astype(F32), jnp.where(ring == OY, ends_ref[1].astype(F32), 1.0)
    )
    wide = lanes(ROWS)

    def laplace(v, cols, f):
        edge = pltpu.roll(cols, B - 2 - 4 * f, 1)
        side = jnp.where(wide == 0, edge, pltpu.roll(v, 1, 1)) + jnp.where(
            wide == B - 1, edge, pltpu.roll(v, B - 1, 1)
        )
        return side + around_rows(v) - 4.0 * v

    for f in range(FLD):
        v = circular(flux_ref, north_ref, south_ref, f)
        once = keep * laplace(v, outer, f)
        twice = laplace(once, beyond, f)
        terms[f] = v[0:OY]
        terms[FLD + f] = once[0:OY]
        terms[2 * FLD + f] = twice[0:OY]

    tall = 32
    copies = []
    for i in range(OY // tall):
        rows = pl.ds(i * tall, tall)
        sea = mask_ref[rows, :].astype(F32)
        held = [terms[j, rows, :] for j in range(3 * FLD)]

        def one(level, carry):
            v = x_ref[level, rows, :]
            for j in range(3 * FLD):
                v = v + coef_ref[j, level] * held[j]
            out_ref[level, rows, :] = v * sea
            return carry

        lax.fori_loop(0, LO, one, 0, unroll=5)
        copies.append(pltpu.make_async_copy(out_ref.at[:, rows], out_hbm.at[:, rows], sems.at[i]))
        copies[-1].start()
    for c in copies:
        c.wait()


def apply_flux(coefs, ends, x, mask, flux, north, south, own, west, east):
    return pl.pallas_call(
        apply_flux_kernel,
        in_specs=[SMEM, SMEM] + [VMEM] * 8,
        out_specs=ANY,
        out_shape=f32(LO, OY, B),
        scratch_shapes=[
            pltpu.VMEM((3 * FLD, OY, B), F32),
            pltpu.VMEM((LO, OY, B), F32),
            pltpu.SemaphoreType.DMA((2,)),
        ],
        compiler_params=params(16),
        name="apply_flux",
    )(coefs, ends, x, mask, flux, north, south, own, west, east)


def swap_rows(low_rows, high_rows):
    count = lax.axis_size("face")
    south_going = [(i, i + 1) for i in range(count - 1)]
    north_going = [(i + 1, i) for i in range(count - 1)]
    north = lax.ppermute(high_rows, "face", south_going)
    south = lax.ppermute(low_rows, "face", north_going)
    return north, south


def swap_columns(for_east, for_west):
    count = lax.axis_size("tile")
    east_going = [(i, (i + 1) % count) for i in range(count)]
    west_going = [((i + 1) % count, i) for i in range(count)]
    west = lax.ppermute(for_east, "tile", east_going)
    east = lax.ppermute(for_west, "tile", west_going)
    return west, east


def exchange(rows):
    return lax.all_to_all(rows, ("face", "tile"), split_axis=0, concat_axis=0, tiled=True)


def mix_levels(v, k):
    flow = k[None, :] * (v[:, 1:] - v[:, :-1])
    return v + jnp.pad(flow, ((0, 0), (0, 1))) - jnp.pad(flow, ((0, 0), (1, 0)))


def local(
    atm_tangent,
    atm_mixing,
    flux_coef,
    remap_weight,
    target_device,
    target_row,
    ocean_tangent,
    ocean_mixing,
    penetration,
    sea_mask,
    ocean_adjoint,
):
    face = lax.axis_index("face")
    ends = jnp.stack([face > 0, face < lax.axis_size("face") - 1]).astype(jnp.int32)
    pen = penetration.T
    north, south = swap_rows(*edge_rows(ocean_adjoint, ocean_tangent, sea_mask))
    pair = surface_flux(flux_coef, atm_tangent, atm_mixing)
    pair, north, south = lax.optimization_barrier((pair, north, south))
    own, for_east, for_west = pack_columns(ocean_adjoint, ocean_tangent, sea_mask, north, south)
    pair, for_east, for_west = lax.optimization_barrier((pair, for_east, for_west))
    west, east = swap_columns(for_east, for_west)
    sent, slots = remap(target_device.T, target_row.T, pair, remap_weight)
    sent, west, east = lax.optimization_barrier((sent, west, east))
    arrived = exchange(sent.reshape(DEV, 1, MSG * B)).reshape(DEV * MSG, B)
    ocean_backward, flux_adjoint = ocean_steps(
        True, ocean_mixing, ends, pen, ocean_adjoint, sea_mask, north, south, own, west, east
    )
    (stepped,) = ocean_steps(
        False, ocean_mixing, ends, pen, ocean_tangent, sea_mask, north, south, own, west, east
    )
    flux_adjoint, stepped = lax.optimization_barrier((flux_adjoint, stepped))
    returned = exchange(answer(arrived, flux_adjoint).reshape(DEV, CAP, FLD, B))
    pen_1 = mix_levels(pen, ocean_mixing)
    pen_2 = mix_levels(pen_1, ocean_mixing)
    coefs = jnp.concatenate([pen_2, (2.0 * HRATE) * pen_1, (HRATE * HRATE) * pen], axis=0)
    flux, low, high = collect(arrived)
    f_north, f_south = swap_rows(low, high)
    f_own, f_sent = flux_columns(flux, f_north, f_south)
    f_west, f_east = swap_columns(f_sent, f_sent)
    ocean_forward = apply_flux(
        coefs, ends, stepped, sea_mask, flux, f_north, f_south, f_own, f_west, f_east
    )
    atm = atm_adjoint(
        slots, flux_coef, returned.reshape(DEV * CAP, FLD, B), atm_mixing, remap_weight
    )
    return ocean_forward, ocean_backward, atm


def solution(mesh):
    placed = (
        P(None, ("face", "tile")),
        P(None, ("face", "tile")),
        P(),
        P(("face", "tile"), None, None),
        P(("face", "tile"), None),
        P(("face", "tile"), None),
        P(None, "face", "tile"),
        P(),
        P(),
        P("face", "tile"),
        P(None, "face", "tile"),
    )
    return jax.shard_map(
        local,
        mesh=mesh,
        in_specs=placed,
        out_specs=(P(None, "face", "tile"), P(None, "face", "tile"), P(None, ("face", "tile"))),
        check_vma=False,
    )
```

profile of v0, /device:TPU:1, one launch (start us, length us, event | category | flops | bytes accessed | tf_op | source)
XLA Modules:
  0.0 101.5 jit_solution(1504953397089087793)
XLA Ops:
  0.6 0.0 copy-start.12
  0.7 0.0 copy-start.2
  0.7 2.3 %edge_rows.1 = (f32[150,2,128]{2,1,0:T(2,128)}, f32[150,2,128]{2,1,0:T(2,128)}) custom-call(f32[75,64,128]{2,1,0:T(8,128)} %x_ref.4, f32[75,64,128]{2,1,0:T(8,128)} %x_ref.5, s32[64,128]{1,0:T(8,128)} %mask_ref.7), custom_call_target="tpu_custom_call" | custom-call | tf_op jit(solution)/shard_map/edge_rows/pallas_call | solution.py:289
  3.0 4.6 %collective-permute-start = (f32[150,2,128]{2,1,0:T(2,128)}, f32[150,2,128]{2,1,0:T(2,128)S(1)}, u32[]{:S(2)}, u32[]{:S(2)}) collective-permute-start(f32[150,2,128]{2,1,0:T(2,128)} %get-tuple-element.28), channel_id=1, source_target_pairs={{0,16},{16,32},{32,48},{48,64},{64,80},{80,96},{96,112},{1,17},{17... | collective-permute-start | bytes 460808 | tf_op jit(solution)/shard_map/ppermute | solution.py:688
  7.6 1.9 %collective-permute-start.1 = (f32[150,2,128]{2,1,0:T(2,128)}, f32[150,2,128]{2,1,0:T(2,128)S(1)}, u32[]{:S(2)}, u32[]{:S(2)}) collective-permute-start(f32[150,2,128]{2,1,0:T(2,128)} %get-tuple-element.29), channel_id=1, source_target_pairs={{16,0},{32,16},{48,32},{64,48},{80,64},{96,80},{112,96},{17,1},{33... | collective-permute-start | bytes 460808 | tf_op jit(solution)/shard_map/ppermute | solution.py:689
  9.5 0.0 copy-start.6
  9.5 1.2 %copy-done.6 = bf16[63,8192]{1,0:T(8,128)(2,1)S(1)} copy-done((bf16[63,8192]{1,0:T(8,128)(2,1)S(1)}, bf16[63,8192]{1,0:T(8,128)(2,1)}, u32[]{:S(2)}) %copy-start.6) | copy-done | bytes 1032216
  10.8 1.6 %copy-done.7 = f32[64,8192]{1,0:T(8,128)S(1)} copy-done((f32[64,8192]{1,0:T(8,128)S(1)}, f32[64,8192]{1,0:T(8,128)}, u32[]{:S(2)}) %copy-start.7) | copy-done | bytes 2097176
  12.3 2.9 %surface_flux.1.pair_ref = f32[512,128]{1,0:T(8,128)S(1)} custom-call(f32[4,64]{1,0:T(4,128)S(1)} %copy-done.12, f32[64,8192]{1,0:T(8,128)S(1)} %copy-done.7, bf16[63,8192]{1,0:T(8,128)(2,1)S(1)} %copy-done.6), custom_call_target="tpu_custom_call" | custom-call | tf_op jit(solution)/shard_map/surface_flux/pallas_call | solution.py:131
  15.2 0.0 copy-start.13
  15.3 0.0 copy-start.14
  15.3 0.0 collective-permute-done.north_ref
  15.3 0.0 collective-permute-done.1.south_ref
  15.3 1.9 %pack_columns.1 = (f32[2,3,72,128]{3,2,1,0:T(8,128)S(1)}, f32[3,72,128]{2,1,0:T(8,128)S(1)}, f32[3,72,128]{2,1,0:T(8,128)S(1)}) custom-call(f32[75,64,128]{2,1,0:T(8,128)S(1)} %copy-done.2, f32[75,64,128]{2,1,0:T(8,128)S(1)} %copy-done.1, s32[64,128]{1,0:T(8,128)S(1)} %copy-done.9, f32[150,2,128]{2,1,0:T(2,128)S(1)} %collective-permute-done.north_ref, ...), custom_call_target="tpu_custom_call" | custom-call | tf_op jit(solution)/shard_map/pack_columns/pallas_call | solution.py:344
  17.2 1.3 %collective-permute-start.2 = (f32[3,72,128]{2,1,0:T(8,128)S(1)}, f32[3,72,128]{2,1,0:T(8,128)S(1)}, u32[]{:S(2)}, u32[]{:S(2)}) collective-permute-start(f32[3,72,128]{2,1,0:T(8,128)S(1)} %get-tuple-element.38), channel_id=1, source_target_pairs={{0,1},{1,2},{2,3},{3,4},{4,5},{5,6},{6,7},{7,8},{8,9},{9,10},{10,1... | collective-permute-start | bytes 331784 | tf_op jit(solution)/shard_map/ppermute | solution.py:697
  18.5 4.8 %collective-permute-start.3 = (f32[3,72,128]{2,1,0:T(8,128)S(1)}, f32[3,72,128]{2,1,0:T(8,128)S(1)}, u32[]{:S(2)}, u32[]{:S(2)}) collective-permute-start(f32[3,72,128]{2,1,0:T(8,128)S(1)} %get-tuple-element.39), channel_id=1, source_target_pairs={{1,0},{2,1},{3,2},{4,3},{5,4},{6,5},{7,6},{8,7},{9,8},{10,9},{11,1... | collective-permute-start | bytes 331784 | tf_op jit(solution)/shard_map/ppermute | solution.py:698
  23.3 0.0 copy-start.11
  23.3 3.2 %remap.1 = (f32[2176,128]{1,0:T(8,128)S(1)}, s32[256]{0:T(256)S(1)}) custom-call(s32[4,64]{1,0:T(4,128)S(1)} %bitcast.16, s32[4,64]{1,0:T(4,128)S(1)} %bitcast.17, f32[512,128]{1,0:T(8,128)S(1)} %surface_flux.1.pair_ref, bf16[256,128,128]{2,1,0:T(8,128)(2,1)S(1)} %copy-done), custom_call_target="tpu_custom_call" | custom-call | tf_op jit(solution)/shard_map/remap/pallas_call | solution.py:180
  26.5 0.0 copy-start.8
  26.5 1.0 copy-done.8
  27.5 0.0 collective-permute-done.2.west_ref
  27.5 0.0 collective-permute-done.3.east_ref
  27.5 8.7 %all-to-all-start = ((f32[128,1,2176]{2,1,0:T(1,128)}), f32[128,1,2176]{2,1,0:T(1,128)}, u32[]{:S(2)}, u32[]{:S(2)}) async-start(f32[128,1,2176]{2,1,0:T(1,128)} %bitcast.12), calls=%async_computation | async-start | bytes 2228224 | tf_op jit(solution)/shard_map/all_to_all | solution.py:703
  36.2 0.1 add_convert_fusion.ends_ref
  36.3 5.1 %ocean_tangent.1.x_ref = f32[75,64,128]{2,1,0:T(8,128)S(1)} custom-call(f32[74]{0:T(128)S(1)} %copy-done.11, s32[2]{0:T(128)S(1)} %add_convert_fusion.ends_ref, f32[4,75]{1,0:T(4,128)S(1)} %bitcast.13, f32[75,64,128]{2,1,0:T(8,128)S(1)} %copy-done.1, s32[64,128]{1,0:T(8,128)S(1)} %copy-done.9, f32[150,2,128]{2,1,0:T(2,128)S(1)} %collective-permute-done.north_ref, ...), custom_call_target="tpu_custom_call" | custom-call | tf_op jit(solution)/shard_map/ocean_tangent/pallas_call | solution.py:507
  41.4 0.0 copy-start.4
  41.4 1.4 %copy-done.4 = f32[75,64,128]{2,1,0:T(8,128)} copy-done((f32[75,64,128]{2,1,0:T(8,128)}, f32[75,64,128]{2,1,0:T(8,128)S(1)}, u32[]{:S(2)}) %copy-start.4) | copy-done | bytes 2457624
  42.8 6.2 %ocean_adjoint.1 = (f32[75,64,128]{2,1,0:T(8,128)}, f32[64,512]{1,0:T(8,128)S(1)}) custom-call(f32[74]{0:T(128)S(1)} %copy-done.11, s32[2]{0:T(128)S(1)} %add_convert_fusion.ends_ref, f32[4,75]{1,0:T(4,128)S(1)} %bitcast.14, f32[75,64,128]{2,1,0:T(8,128)S(1)} %copy-done.3, s32[64,128]{1,0:T(8,128)S(1)} %copy-done.9, ...), custom_call_target="tpu_custom_call" | custom-call | tf_op jit(solution)/shard_map/ocean_adjoint/pallas_call | solution.py:507
  49.1 6.5 %all-to-all-done = f32[128,1,2176]{2,1,0:T(1,128)} async-done(((f32[128,1,2176]{2,1,0:T(1,128)}), f32[128,1,2176]{2,1,0:T(1,128)}, u32[]{:S(2)}, u32[]{:S(2)}) %all-to-all-start) | async-done | bytes 1114144 | tf_op jit(solution)/shard_map/all_to_all | solution.py:703
  55.5 2.9 %answer.1 = f32[2048,128]{1,0:T(8,128)} custom-call(f32[2176,128]{1,0:T(8,128)} %bitcast.6.msg_ref, f32[64,512]{1,0:T(8,128)S(1)} %get-tuple-element.52.flux_ref), custom_call_target="tpu_custom_call" | custom-call | tf_op jit(solution)/shard_map/answer/pallas_call | solution.py:549
  58.4 5.7 %all-to-all-start.1 = ((f32[128,4,4,128]{3,2,1,0:T(4,128)}), f32[128,4,4,128]{3,2,1,0:T(4,128)}, u32[]{:S(2)}, u32[]{:S(2)}) async-start(f32[128,4,4,128]{3,2,1,0:T(4,128)} %bitcast.7), calls=%async_computation.1 | async-start | bytes 2097152 | tf_op jit(solution)/shard_map/all_to_all | solution.py:703
  64.1 0.1 subtract_multiply_fusion.1
  64.2 0.1 broadcast_multiply_fusion.1
  64.2 0.1 subtract_multiply_fusion
  64.3 1.6 %collect.1 = (f32[4,64,128]{2,1,0:T(8,128)S(1)}, f32[4,2,128]{2,1,0:T(2,128)S(1)}, f32[4,2,128]{2,1,0:T(2,128)S(1)}) custom-call(f32[2176,128]{1,0:T(8,128)} %bitcast.6.msg_ref), custom_call_target="tpu_custom_call" | custom-call | tf_op jit(solution)/shard_map/collect/pallas_call | solution.py:576
  65.9 3.6 %collective-permute-start.4 = (f32[4,2,128]{2,1,0:T(2,128)S(1)}, f32[4,2,128]{2,1,0:T(2,128)S(1)}, u32[]{:S(2)}, u32[]{:S(2)}) collective-permute-start(f32[4,2,128]{2,1,0:T(2,128)S(1)} %get-tuple-element.46), channel_id=1, source_target_pairs={{0,16},{16,32},{32,48},{48,64},{64,80},{80,96},{96,112},{1,17},{17... | collective-permute-start | bytes 12296 | tf_op jit(solution)/shard_map/ppermute | solution.py:688
  69.5 1.9 %collective-permute-start.5 = (f32[4,2,128]{2,1,0:T(2,128)S(1)}, f32[4,2,128]{2,1,0:T(2,128)S(1)}, u32[]{:S(2)}, u32[]{:S(2)}) collective-permute-start(f32[4,2,128]{2,1,0:T(2,128)S(1)} %get-tuple-element.47), channel_id=1, source_target_pairs={{16,0},{32,16},{48,32},{64,48},{80,64},{96,80},{112,96},{17,1},{33... | collective-permute-start | bytes 12296 | tf_op jit(solution)/shard_map/ppermute | solution.py:689
  71.4 0.1 pad_subtract_fusion
  71.5 0.0 collective-permute-done.4.north_ref
  71.5 3.4 %collective-permute-done.5.south_ref = f32[4,2,128]{2,1,0:T(2,128)S(1)} collective-permute-done((f32[4,2,128]{2,1,0:T(2,128)S(1)}, f32[4,2,128]{2,1,0:T(2,128)S(1)}, u32[]{:S(2)}, u32[]{:S(2)}) %collective-permute-start.5) | collective-permute-done | bytes 4128 | tf_op jit(solution)/shard_map/ppermute | solution.py:689
  74.9 0.2 flux_columns.1
  75.1 7.0 %collective-permute-start.7 = (f32[16,128]{1,0:T(8,128)S(1)}, f32[16,128]{1,0:T(8,128)S(1)}, u32[]{:S(2)}, u32[]{:S(2)}) collective-permute-start(f32[16,128]{1,0:T(8,128)S(1)} %get-tuple-element.49), channel_id=1, source_target_pairs={{1,0},{2,1},{3,2},{4,3},{5,4},{6,5},{7,6},{8,7},{9,8},{10,9},{11,1... | collective-permute-start | bytes 24584 | tf_op jit(solution)/shard_map/ppermute | solution.py:698
  82.0 0.0 collective-permute-start.6
  82.1 0.8 collective-permute-done.7.east_ref
  82.8 5.0 %collective-permute-done.6.west_ref = f32[16,128]{1,0:T(8,128)S(1)} collective-permute-done((f32[16,128]{1,0:T(8,128)S(1)}, f32[16,128]{1,0:T(8,128)S(1)}, u32[]{:S(2)}, u32[]{:S(2)}) %collective-permute-start.6) | collective-permute-done | bytes 8224 | tf_op jit(solution)/shard_map/ppermute | solution.py:697
  87.9 4.8 %apply_flux.1 = f32[75,64,128]{2,1,0:T(8,128)} custom-call(f32[12,75]{1,0:T(8,128)S(1)} %pad_maximum_fusion.coef_ref, s32[2]{0:T(128)S(1)} %add_convert_fusion.ends_ref, f32[75,64,128]{2,1,0:T(8,128)S(1)} %copy-done.5, s32[64,128]{1,0:T(8,128)S(1)} %copy-done.9, f32[4,64,128]{2,1,0:T(8,128)S(1)} %get-tuple-element.45.flux_ref, ...), custom_call_target="tpu_custom_call" | custom-call | tf_op jit(solution)/shard_map/apply_flux/pallas_call | solution.py:669
  92.7 0.0 all-to-all-done.1
  92.7 8.8 %atm_adjoint.1 = f32[64,8192]{1,0:T(8,128)} custom-call(s32[256]{0:T(256)} %copy-done.15, f32[4,64]{1,0:T(4,128)} %coef_ref.3, f32[512,4,128]{2,1,0:T(4,128)} %bitcast.8.back_ref, bf16[63,8192]{1,0:T(8,128)(2,1)} %mix_ref.3, bf16[256,128,128]{2,1,0:T(8,128)(2,1)} %w_hbm.1), custom_call_target="tpu_custom_call" | custom-call | tf_op jit(solution)/shard_map/atm_adjoint/pallas_call | solution.py:251
  (21 shorter events, 0.0 us)
Async XLA Ops:
  0.6 8.9 %copy-start.12 = (f32[4,64]{1,0:T(4,128)S(1)}, f32[4,64]{1,0:T(4,128)}, u32[]{:S(2)}) copy-start(f32[4,64]{1,0:T(4,128)} %coef_ref.3) | copy-start | bytes 3076
  0.6 14.6 %copy-start.1 = (f32[75,64,128]{2,1,0:T(8,128)S(1)}, f32[75,64,128]{2,1,0:T(8,128)}, u32[]{:S(2)}) copy-start(f32[75,64,128]{2,1,0:T(8,128)} %x_ref.5) | copy-start | bytes 7372804
  0.7 14.6 %copy-start.2 = (f32[75,64,128]{2,1,0:T(8,128)S(1)}, f32[75,64,128]{2,1,0:T(8,128)}, u32[]{:S(2)}) copy-start(f32[75,64,128]{2,1,0:T(8,128)} %x_ref.4) | copy-start | bytes 7372804
  0.7 14.6 %copy-start.9 = (s32[64,128]{1,0:T(8,128)S(1)}, s32[64,128]{1,0:T(8,128)}, u32[]{:S(2)}) copy-start(s32[64,128]{1,0:T(8,128)} %mask_ref.7) | copy-start | bytes 98308
  3.0 12.3 %collective-permute-start = (f32[150,2,128]{2,1,0:T(2,128)}, f32[150,2,128]{2,1,0:T(2,128)S(1)}, u32[]{:S(2)}, u32[]{:S(2)}) collective-permute-start(f32[150,2,128]{2,1,0:T(2,128)} %get-tuple-element.28), channel_id=1, source_target_pairs={{0,16},{16,32},{32,48},{48,64},{64,80},{80,96},{96,112},{1,17},{17... | collective-permute-start | bytes 460808 | tf_op jit(solution)/shard_map/ppermute | solution.py:688
  7.6 7.7 %collective-permute-start.1 = (f32[150,2,128]{2,1,0:T(2,128)}, f32[150,2,128]{2,1,0:T(2,128)S(1)}, u32[]{:S(2)}, u32[]{:S(2)}) collective-permute-start(f32[150,2,128]{2,1,0:T(2,128)} %get-tuple-element.29), channel_id=1, source_target_pairs={{16,0},{32,16},{48,32},{64,48},{80,64},{96,80},{112,96},{17,1},{33... | collective-permute-start | bytes 460808 | tf_op jit(solution)/shard_map/ppermute | solution.py:689
  9.5 1.2 %copy-start.6 = (bf16[63,8192]{1,0:T(8,128)(2,1)S(1)}, bf16[63,8192]{1,0:T(8,128)(2,1)}, u32[]{:S(2)}) copy-start(bf16[63,8192]{1,0:T(8,128)(2,1)} %mix_ref.3) | copy-start | bytes 3096580
  10.7 1.6 %copy-start.7 = (f32[64,8192]{1,0:T(8,128)S(1)}, f32[64,8192]{1,0:T(8,128)}, u32[]{:S(2)}) copy-start(f32[64,8192]{1,0:T(8,128)} %x_ref.3) | copy-start | bytes 6291460
  12.3 10.9 %copy-start = (bf16[256,128,128]{2,1,0:T(8,128)(2,1)S(1)}, bf16[256,128,128]{2,1,0:T(8,128)(2,1)}, u32[]{:S(2)}) copy-start(bf16[256,128,128]{2,1,0:T(8,128)(2,1)} %w_hbm.1) | copy-start | bytes 25165828
  15.2 8.0 %copy-start.13 = (s32[64,4]{0,1:T(4,128)S(1)}, s32[64,4]{0,1:T(4,128)}, u32[]{:S(2)}) copy-start(s32[64,4]{0,1:T(4,128)} %param.15) | copy-start | bytes 3076
  15.3 8.0 %copy-start.14 = (s32[64,4]{0,1:T(4,128)S(1)}, s32[64,4]{0,1:T(4,128)}, u32[]{:S(2)}) copy-start(s32[64,4]{0,1:T(4,128)} %param.16) | copy-start | bytes 3076
  17.2 10.3 %collective-permute-start.2 = (f32[3,72,128]{2,1,0:T(8,128)S(1)}, f32[3,72,128]{2,1,0:T(8,128)S(1)}, u32[]{:S(2)}, u32[]{:S(2)}) collective-permute-start(f32[3,72,128]{2,1,0:T(8,128)S(1)} %get-tuple-element.38), channel_id=1, source_target_pairs={{0,1},{1,2},{2,3},{3,4},{4,5},{5,6},{6,7},{7,8},{8,9},{9,10},{10,1... | collective-permute-start | bytes 331784 | tf_op jit(solution)/shard_map/ppermute | solution.py:697
  18.5 9.0 %collective-permute-start.3 = (f32[3,72,128]{2,1,0:T(8,128)S(1)}, f32[3,72,128]{2,1,0:T(8,128)S(1)}, u32[]{:S(2)}, u32[]{:S(2)}) collective-permute-start(f32[3,72,128]{2,1,0:T(8,128)S(1)} %get-tuple-element.39), channel_id=1, source_target_pairs={{1,0},{2,1},{3,2},{4,3},{5,4},{6,5},{7,6},{8,7},{9,8},{10,9},{11,1... | collective-permute-start | bytes 331784 | tf_op jit(solution)/shard_map/ppermute | solution.py:698
  23.3 13.0 %copy-start.10 = (f32[75,4]{0,1:T(4,128)S(1)}, f32[75,4]{0,1:T(4,128)}, u32[]{:S(2)}) copy-start(f32[75,4]{0,1:T(4,128)} %param.19) | copy-start | bytes 3604
  23.3 13.0 %copy-start.11 = (f32[74]{0:T(128)S(1)}, f32[74]{0:T(128)}, u32[]{:S(2)}) copy-start(f32[74]{0:T(128)} %k_ref.3) | copy-start | bytes 892
  26.5 1.0 copy-start.8
  27.5 8.8 %copy-start.15 = (s32[256]{0:T(256)}, s32[256]{0:T(256)S(1)}, u32[]{:S(2)}) copy-start(s32[256]{0:T(256)S(1)} %get-tuple-element.51.slot_ref) | copy-start | bytes 3076
  27.5 28.0 %all-to-all-start = ((f32[128,1,2176]{2,1,0:T(1,128)}), f32[128,1,2176]{2,1,0:T(1,128)}, u32[]{:S(2)}, u32[]{:S(2)}) async-start(f32[128,1,2176]{2,1,0:T(1,128)} %bitcast.12), calls=%async_computation | async-start | bytes 2228224 | tf_op jit(solution)/shard_map/all_to_all | solution.py:703
  36.3 6.6 %copy-start.3 = (f32[75,64,128]{2,1,0:T(8,128)S(1)}, f32[75,64,128]{2,1,0:T(8,128)}, u32[]{:S(2)}) copy-start(f32[75,64,128]{2,1,0:T(8,128)} %x_ref.4) | copy-start | bytes 7372804
  41.4 1.4 %copy-start.4 = (f32[75,64,128]{2,1,0:T(8,128)}, f32[75,64,128]{2,1,0:T(8,128)S(1)}, u32[]{:S(2)}) copy-start(f32[75,64,128]{2,1,0:T(8,128)S(1)} %ocean_tangent.1.x_ref) | copy-start | bytes 7372804
  55.5 32.4 %copy-start.5 = (f32[75,64,128]{2,1,0:T(8,128)S(1)}, f32[75,64,128]{2,1,0:T(8,128)}, u32[]{:S(2)}) copy-start(f32[75,64,128]{2,1,0:T(8,128)} %copy-done.4) | copy-start | bytes 7372804
  58.4 34.3 %all-to-all-start.1 = ((f32[128,4,4,128]{3,2,1,0:T(4,128)}), f32[128,4,4,128]{3,2,1,0:T(4,128)}, u32[]{:S(2)}, u32[]{:S(2)}) async-start(f32[128,4,4,128]{3,2,1,0:T(4,128)} %bitcast.7), calls=%async_computation.1 | async-start | bytes 2097152 | tf_op jit(solution)/shard_map/all_to_all | solution.py:703
  65.9 5.6 %collective-permute-start.4 = (f32[4,2,128]{2,1,0:T(2,128)S(1)}, f32[4,2,128]{2,1,0:T(2,128)S(1)}, u32[]{:S(2)}, u32[]{:S(2)}) collective-permute-start(f32[4,2,128]{2,1,0:T(2,128)S(1)} %get-tuple-element.46), channel_id=1, source_target_pairs={{0,16},{16,32},{32,48},{48,64},{64,80},{80,96},{96,112},{1,17},{17... | collective-permute-start | bytes 12296 | tf_op jit(solution)/shard_map/ppermute | solution.py:688
  69.5 5.4 %collective-permute-start.5 = (f32[4,2,128]{2,1,0:T(2,128)S(1)}, f32[4,2,128]{2,1,0:T(2,128)S(1)}, u32[]{:S(2)}, u32[]{:S(2)}) collective-permute-start(f32[4,2,128]{2,1,0:T(2,128)S(1)} %get-tuple-element.47), channel_id=1, source_target_pairs={{16,0},{32,16},{48,32},{64,48},{80,64},{96,80},{112,96},{17,1},{33... | collective-permute-start | bytes 12296 | tf_op jit(solution)/shard_map/ppermute | solution.py:689
  75.1 7.8 %collective-permute-start.7 = (f32[16,128]{1,0:T(8,128)S(1)}, f32[16,128]{1,0:T(8,128)S(1)}, u32[]{:S(2)}, u32[]{:S(2)}) collective-permute-start(f32[16,128]{1,0:T(8,128)S(1)} %get-tuple-element.49), channel_id=1, source_target_pairs={{1,0},{2,1},{3,2},{4,3},{5,4},{6,5},{7,6},{8,7},{9,8},{10,9},{11,1... | collective-permute-start | bytes 24584 | tf_op jit(solution)/shard_map/ppermute | solution.py:698
  82.0 5.8 %collective-permute-start.6 = (f32[16,128]{1,0:T(8,128)S(1)}, f32[16,128]{1,0:T(8,128)S(1)}, u32[]{:S(2)}, u32[]{:S(2)}) collective-permute-start(f32[16,128]{1,0:T(8,128)S(1)} %get-tuple-element.49), channel_id=1, source_target_pairs={{0,1},{1,2},{2,3},{3,4},{4,5},{5,6},{6,7},{7,8},{8,9},{9,10},{10,1... | collective-permute-start | bytes 24584 | tf_op jit(solution)/shard_map/ppermute | solution.py:697
where the time goes:
time: 102 us
  Pallas kernels  39.8 us (39%)
  starting transfers between devices  39.4 us (39%)
  waiting for transfers between devices  15.7 us (15%)
  local copies, waits for them, and re-layouts  5.29 us (5%)
    all_to_all x2, starting transfers between devices, exchange(): lax.all_to_all(rows, ('face', 'tile'), split_axis=0, concat_axis=0, tiled...  14.3 us
    ppermute x2, starting transfers between devices, swap_columns(): east = lax.ppermute(for_west, 'tile', west_going)  11.8 us
    pallas_call x2, Pallas kernels, ocean_steps(): pl.pallas_call(functools.partial(ocean_kernel, adjoint), grid=(1,), in_sp...  11.3 us
    pallas_call x1, Pallas kernels, atm_adjoint(): pl.pallas_call(atm_adjoint_kernel, in_specs=[SMEM, SMEM, VMEM, VMEM, ANY]...  8.83 us
    ppermute x2, starting transfers between devices, swap_rows(): north = lax.ppermute(high_rows, 'face', south_going)  8.19 us
    all_to_all x2, waiting for transfers between devices, exchange(): lax.all_to_all(rows, ('face', 'tile'), split_axis=0, concat_axis=0, tiled...  6.45 us
    unnamed x32, local copies, waits for them, and re-layouts  5.29 us
    ppermute x2, waiting for transfers between devices, swap_columns(): west = lax.ppermute(for_east, 'tile', east_going)  5.03 us
  transfers between devices with their start and end apart: 10, of which 4 were waited for; matrix products, arithmetic and copies ran while one was open for 0% of the time, Pallas kernels for 24%

commit v1 on v0

--- a/solution.py
+++ b/solution.py
@@ -19,6 +19,8 @@
 CAP = 4
 DEV = 128
 MSG = CAP * FLD + 1
+PIECES = 64
+LOT = KO * FLD + 1
 GRP = 8
 STEPS = NBA // GRP
 PLANES = 3
@@ -33,11 +35,14 @@
 VMEM = pl.BlockSpec(memory_space=pltpu.VMEM)
 ANY = pl.BlockSpec(memory_space=pl.ANY)
 PITCH = LA + 1
-ALONE = 58
 
 
 def params(mib):
     return pltpu.CompilerParams(vmem_limit_bytes=mib * MIB)
+
+
+def in_hbm(v):
+    return pltpu.with_memory_space_constraint(v, pltpu.HBM)
 
 
 def f32(*shape):
@@ -139,7 +144,51 @@
     )(coef, x, mix)
 
 
-def remap_kernel(td_ref, tr_ref, pair_ref, w_ref, out_ref, slot_ref, count):
+def columns_of(rows):
+    count, length = rows.shape
+    wide = jnp.concatenate([rows, jnp.zeros((count, B - length), F32)], axis=1)
+    return jnp.concatenate([wide, jnp.zeros((B - count, B), F32)], axis=0).T[0:length]
+
+
+def label_rows(td_ref, tr_ref, parts, tiles):
+    dev = td_ref[...]
+    dev_cols = columns_of(dev.astype(F32))
+    row_cols = columns_of(tr_ref[...].astype(F32) + 1.0)
+    east = dev // tiles * tiles + (dev + 1) % tiles
+    west = dev // tiles * tiles + (dev + tiles - 1) % tiles
+    lane = lanes(NBA)
+    earlier = (
+        lax.broadcasted_iota(jnp.int32, (NBA, NBA), 1) < lax.broadcasted_iota(jnp.int32, (NBA, NBA), 0)
+    )
+    owner = lax.broadcasted_iota(jnp.int32, (DEV, NBA), 0)
+    total = jnp.zeros((DEV, B), F32)
+    for k in range(KO):
+        mine = dev_cols[:, k : k + 1]
+        same = jnp.zeros((NBA, NBA), F32)
+        for other in range(KO):
+            same = same + (mine == dev[other : other + 1].astype(F32)).astype(F32)
+        place = jnp.sum(jnp.where(earlier, same, 0.0), axis=1, keepdims=True).astype(jnp.int32)
+        label = row_cols[:, k : k + 1]
+        piece = jnp.zeros((NBA, B), F32)
+        for f in range(FLD):
+            v = parts[pl.ds(k * FLD + f, NBA, stride=LOT), :]
+            piece = jnp.where(lane // 4 == f, pltpu.roll(v, 4 * f + 2, 1), piece)
+        piece = piece + pltpu.roll(piece, 16, 1)
+        piece = pltpu.roll(piece + pltpu.roll(piece, 32, 1), PIECES, 1)
+        piece = jnp.where(lane // 16 == PIECES // 16 + place, piece, 0.0)
+        own = jnp.where(lane == place, label, 0.0)
+        to_east = jnp.where(lane == 4 + place, label, jnp.where(lane % 4 < 2, piece, 0.0))
+        to_west = jnp.where(lane == 8 + place, label, jnp.where(lane % 4 < 2, 0.0, piece))
+        picks = [
+            (owner == d[k : k + 1]).astype(F32).astype(BF16) for d in (dev, east, west)
+        ]
+        hi, lo = split2(jnp.concatenate([own, to_east, to_west], axis=0))
+        pick = jnp.concatenate(picks, axis=1)
+        total = total + dot(pick, hi) + dot(pick, lo)
+    return total
+
+
+def remap_kernel(tiles, td_ref, td_rows, tr_rows, pair_ref, w_ref, out_ref, slot_ref, count, parts):
     out_ref[...] = jnp.zeros_like(out_ref)
 
     def clear(d, c):
@@ -147,7 +196,6 @@
         return c
 
     lax.fori_loop(0, DEV, clear, 0, unroll=8)
-    lane = lanes(1)
     upper = lax.broadcasted_iota(jnp.int32, (4 * FLD, B), 0) < 2 * FLD
 
     def work(step, carry):
@@ -157,35 +205,38 @@
             lhs = jnp.concatenate(
                 [jnp.where(upper, both, 0.0), jnp.where(upper, 0.0, both)], axis=1
             ).astype(BF16)
+            ats = {}
+            for a in range(2):
+                for k in range(KO):
+                    dev = td_ref[k, row + a]
+                    place = count[dev]
+                    count[dev] = place + 1
+                    slot_ref[(row + a) * KO + k] = dev * CAP + place
+                    ats[a, k] = dev * MSG + place * FLD
             for k in range(0, KO, 2):
                 moved = dot(lhs, square(w_ref, row, k))
                 for a in range(2):
                     total = moved[8 * a : 8 * a + 4] + moved[8 * a + 4 : 8 * a + 8]
                     for b in range(2):
-                        dev = td_ref[k + b, row + a]
-                        place = count[dev]
-                        count[dev] = place + 1
-                        slot_ref[(row + a) * KO + k + b] = dev * CAP + place
-                        at = dev * MSG
-                        out_ref[pl.ds(at + place * FLD, FLD), :] = total[:, b * B : (b + 1) * B]
-                        label = (tr_ref[k + b, row + a] + 1).astype(F32)
-                        last = pl.ds(at + MSG - 1, 1)
-                        out_ref[last, :] = jnp.where(lane == place, label, out_ref[last, :])
+                        half = total[:, b * B : (b + 1) * B]
+                        out_ref[pl.ds(ats[a, k + b], FLD), :] = half
+                        parts[pl.ds((row + a) * LOT + (k + b) * FLD, FLD), :] = half
         return carry
 
     lax.fori_loop(0, STEPS, work, 0, unroll=STEPS)
-
-
-def remap(td, tr, pair, w):
+    out_ref[pl.ds(MSG - 1, DEV, stride=MSG), :] = label_rows(td_rows, tr_rows, parts, tiles)
+
+
+def remap(tiles, td, tr, pair, w):
     return pl.pallas_call(
-        remap_kernel,
-        in_specs=[SMEM, SMEM, VMEM, VMEM],
+        functools.partial(remap_kernel, tiles),
+        in_specs=[SMEM] + [VMEM] * 4,
         out_specs=[VMEM, SMEM],
-        out_shape=[f32(DEV * MSG, B), jax.ShapeDtypeStruct((NBA * KO,), jnp.int32)],
-        scratch_shapes=[pltpu.SMEM((DEV,), jnp.int32)],
+        out_shape=[pltpu.HBM((DEV * MSG, B), F32), jax.ShapeDtypeStruct((NBA * KO,), jnp.int32)],
+        scratch_shapes=[pltpu.SMEM((DEV,), jnp.int32), pltpu.VMEM((NBA * LOT, B), F32)],
         compiler_params=params(16),
         name="remap",
-    )(td, tr, pair, w)
+    )(td, td, tr, pair, w)
 
 
 def atm_adjoint_kernel(
@@ -261,9 +312,9 @@
             pltpu.VMEM((LA, NBA * B), F32),
             pltpu.SemaphoreType.DMA((2, STEPS)),
         ],
-        compiler_params=params(ALONE),
+        compiler_params=params(24),
         name="atm_adjoint",
-    )(slots, coef, back, mix, w)
+    )(slots, coef, back, mix, in_hbm(w))
 
 
 def rows_kernel(a_hbm, t_hbm, m_hbm, low_ref, high_ref, a_ref, t_ref, m_ref, sems):
@@ -297,9 +348,9 @@
             pltpu.VMEM((2, 8, B), jnp.int32),
             pltpu.SemaphoreType.DMA((3, 2)),
         ],
-        compiler_params=params(ALONE),
+        compiler_params=params(8),
         name="edge_rows",
-    )(adjoint, tangent, mask)
+    )(in_hbm(adjoint), in_hbm(tangent), in_hbm(mask))
 
 
 def level_lanes(plane):
@@ -554,71 +605,68 @@
     )(msg, flux)
 
 
-def collect_kernel(msg_ref, flux_ref, low_ref, high_ref):
-    labels = msg_ref[pl.ds(MSG - 1, DEV, stride=MSG), :].T.astype(jnp.int32)
+def collect_kernel(msg_ref, flux_ref, outer_ref, low_ref, high_ref):
+    last = msg_ref[pl.ds(MSG - 1, DEV, stride=MSG), :]
+    labels = last.T.astype(jnp.int32)
     rows = lax.broadcasted_iota(jnp.int32, (OY, DEV), 0) + 1
+
+    def picked(at):
+        return (labels[at : at + 1, :] == rows).astype(F32).astype(BF16)
+
+    lane = lanes(DEV)
+    first_lot = lane < 4 * FLD
     total = jnp.zeros((OY, FLD * B), F32)
+    outer = jnp.zeros((OY, B), F32)
     for c in range(CAP):
-        pick = (labels[c : c + 1, :] == rows).astype(F32).astype(BF16)
+        pick = picked(c)
         data = jnp.concatenate(
             [msg_ref[pl.ds(c * FLD + f, DEV, stride=MSG), :] for f in range(FLD)], axis=1
         )
         dh, dl = split2(data)
         total = total + dot(jnp.concatenate([pick, pick], axis=1), jnp.concatenate([dh, dl], axis=0))
+        piece = jnp.where(first_lot, pltpu.roll(last, (2 * B - PIECES - 16 * c) % B, 1), 0.0)
+        west = jnp.where(lane % 4 < 2, piece, 0.0)
+        wh, wl = split2(west)
+        eh, el = split2(piece - west)
+        west_pick, east_pick = picked(4 + c), picked(8 + c)
+        outer = outer + dot(
+            jnp.concatenate([west_pick, west_pick, east_pick, east_pick], axis=1),
+            jnp.concatenate([wh, wl, eh, el], axis=0),
+        )
+    outer_ref[...] = outer
     for f in range(FLD):
         v = total[:, f * B : (f + 1) * B]
         flux_ref[f] = v
         low_ref[f] = v[0:2]
         high_ref[f] = v[OY - 2 : OY]
+    low_ref[FLD] = outer[0:2]
+    high_ref[FLD] = outer[OY - 2 : OY]
 
 
 def collect(msg):
     return pl.pallas_call(
         collect_kernel,
-        out_shape=[f32(FLD, OY, B), f32(FLD, 2, B), f32(FLD, 2, B)],
+        out_shape=[f32(FLD, OY, B), f32(OY, B), f32(FLD + 1, 2, B), f32(FLD + 1, 2, B)],
         compiler_params=params(12),
         name="collect",
     )(msg)
 
 
-def circular(flux_ref, north_ref, south_ref, f):
-    return jnp.concatenate(
-        [flux_ref[f], south_ref[f], jnp.zeros((ROWS - OY - 4, B), F32), north_ref[f]], axis=0
-    )
-
-
-def flux_columns_kernel(flux_ref, north_ref, south_ref, own_ref, out_ref):
-    lane = lanes(1)
-    held = jnp.zeros((ROWS, B), F32)
-    for f in range(FLD):
-        v = circular(flux_ref, north_ref, south_ref, f)
-        held = jnp.where(lane // 4 == f, pltpu.roll(v, 4 * f + 2, 1), held)
-    own_ref[...] = held
-    square = jnp.concatenate([held, jnp.zeros((B - ROWS, B), F32)], axis=0)
-    out_ref[...] = square.T[0 : 4 * FLD]
-
-
-def flux_columns(flux, north, south):
-    return pl.pallas_call(
-        flux_columns_kernel,
-        out_shape=[f32(ROWS, B), f32(4 * FLD, B)],
-        compiler_params=params(12),
-        name="flux_columns",
-    )(flux, north, south)
-
-
-def unsent(ref):
-    return jnp.concatenate([ref[...], jnp.zeros((B - 4 * FLD, B), F32)], axis=0).T[0:ROWS]
+def circular(own, north, south):
+    return jnp.concatenate([own, south, jnp.zeros((ROWS - OY - 4, B), F32), north], axis=0)
 
 
 def apply_flux_kernel(
-    coef_ref, ends_ref, x_ref, mask_ref, flux_ref, north_ref, south_ref, own_ref, west_ref, east_ref,
+    coef_ref, ends_ref, x_ref, mask_ref, flux_ref, outer_ref, north_ref, south_ref,
     out_hbm, terms, out_ref, sems
 ):
     lane = lanes(1)
     part = lane % 4
-    own = own_ref[...]
-    outer = jnp.where(part < 2, unsent(west_ref), unsent(east_ref))
+    planes = [circular(flux_ref[f], north_ref[f], south_ref[f]) for f in range(FLD)]
+    own = jnp.zeros((ROWS, B), F32)
+    for f in range(FLD):
+        own = jnp.where(lane // 4 == f, pltpu.roll(planes[f], 4 * f + 2, 1), own)
+    outer = circular(outer_ref[...], north_ref[FLD], south_ref[FLD])
     from_west = jnp.where(part == 1, pltpu.roll(outer, 1, 1), pltpu.roll(own, 1, 1))
     from_east = jnp.where(part == 1, pltpu.roll(own, B - 1, 1), pltpu.roll(outer, B - 1, 1))
     beyond = from_west + from_east + around_rows(outer) - 4.0 * outer
@@ -637,7 +685,7 @@
         return side + around_rows(v) - 4.0 * v
 
     for f in range(FLD):
-        v = circular(flux_ref, north_ref, south_ref, f)
+        v = planes[f]
         once = keep * laplace(v, outer, f)
         twice = laplace(once, beyond, f)
         terms[f] = v[0:OY]
@@ -665,10 +713,10 @@
         c.wait()
 
 
-def apply_flux(coefs, ends, x, mask, flux, north, south, own, west, east):
+def apply_flux(coefs, ends, x, mask, flux, outer, north, south):
     return pl.pallas_call(
         apply_flux_kernel,
-        in_specs=[SMEM, SMEM] + [VMEM] * 8,
+        in_specs=[SMEM, SMEM] + [VMEM] * 6,
         out_specs=ANY,
         out_shape=f32(LO, OY, B),
         scratch_shapes=[
@@ -678,7 +726,7 @@
         ],
         compiler_params=params(16),
         name="apply_flux",
-    )(coefs, ends, x, mask, flux, north, south, own, west, east)
+    )(coefs, ends, x, mask, flux, outer, north, south)
 
 
 def swap_rows(low_rows, high_rows):
@@ -730,7 +778,9 @@
     own, for_east, for_west = pack_columns(ocean_adjoint, ocean_tangent, sea_mask, north, south)
     pair, for_east, for_west = lax.optimization_barrier((pair, for_east, for_west))
     west, east = swap_columns(for_east, for_west)
-    sent, slots = remap(target_device.T, target_row.T, pair, remap_weight)
+    sent, slots = remap(
+        lax.axis_size("tile"), target_device.T, target_row.T, pair, remap_weight
+    )
     sent, west, east = lax.optimization_barrier((sent, west, east))
     arrived = exchange(sent.reshape(DEV, 1, MSG * B)).reshape(DEV * MSG, B)
     ocean_backward, flux_adjoint = ocean_steps(
@@ -744,13 +794,9 @@
     pen_1 = mix_levels(pen, ocean_mixing)
     pen_2 = mix_levels(pen_1, ocean_mixing)
     coefs = jnp.concatenate([pen_2, (2.0 * HRATE) * pen_1, (HRATE * HRATE) * pen], axis=0)
-    flux, low, high = collect(arrived)
+    flux, outer, low, high = collect(arrived)
     f_north, f_south = swap_rows(low, high)
-    f_own, f_sent = flux_columns(flux, f_north, f_south)
-    f_west, f_east = swap_columns(f_sent, f_sent)
-    ocean_forward = apply_flux(
-        coefs, ends, stepped, sea_mask, flux, f_north, f_south, f_own, f_west, f_east
-    )
+    ocean_forward = apply_flux(coefs, ends, stepped, sea_mask, flux, outer, f_north, f_south)
     atm = atm_adjoint(
         slots, flux_coef, returned.reshape(DEV * CAP, FLD, B), atm_mixing, remap_weight
     )

time: 102 us -> 91.5 us (0.90)
  starting transfers between devices: 39.4 us -> 32.6 us
  waiting for transfers between devices: 15.7 us -> 13.1 us
    ppermute x2 -> x1, starting transfers between devices: 11.8 us -> 4.82 us  [swap_columns(): east = lax.ppermute(for_west, 'tile', west_going)]
    ppermute x2 -> x1, waiting for transfers between devices: 5.03 us -> 0.01 us  [swap_columns(): west = lax.ppermute(for_east, 'tile', east_going)]
    all_to_all x2, waiting for transfers between devices: 6.45 us -> 9.62 us  [exchange(): lax.all_to_all(rows, ('face', 'tile'), split_axis=0, concat_axis=0, tiled...]
    pallas_call x4 -> x3, Pallas kernels: 9.71 us -> 10.7 us  [the longest x1 4.87 us: apply_flux(): pl.pallas_call(apply_flux_kernel, in_specs=[SMEM, SMEM] + [VMEM] * 6, out...]
    unnamed x32 -> x30, local copies, waits for them, and re-layouts: 5.29 us -> 4.3 us
  transfers between devices with their start and end apart: 10 -> 8, of which waited for: 4 -> 3; matrix products, arithmetic and copies ran while one was open for 0% -> 0% of each run, Pallas kernels for 24% -> 27%
where the time goes in v1:
time: 91.5 us; the launch traced here: 91.1 us
  Pallas kernels  39.8 us (43%)
  starting transfers between devices  32.6 us (36%)
  waiting for transfers between devices  13.1 us (14%)
  local copies, waits for them, and re-layouts  4.3 us (5%)
    all_to_all x2, starting transfers between devices, exchange(): lax.all_to_all(rows, ('face', 'tile'), split_axis=0, concat_axis=0, tiled...  14.3 us
    pallas_call x2, Pallas kernels, ocean_steps(): pl.pallas_call(functools.partial(ocean_kernel, adjoint), grid=(1,), in_sp...  11.3 us
    all_to_all x2, waiting for transfers between devices, exchange(): lax.all_to_all(rows, ('face', 'tile'), split_axis=0, concat_axis=0, tiled...  9.62 us
    pallas_call x1, Pallas kernels, atm_adjoint(): pl.pallas_call(atm_adjoint_kernel, in_specs=[SMEM, SMEM, VMEM, VMEM, ANY]...  8.51 us
    ppermute x2, starting transfers between devices, swap_rows(): north = lax.ppermute(high_rows, 'face', south_going)  8.33 us
    pallas_call x1, Pallas kernels, apply_flux(): pl.pallas_call(apply_flux_kernel, in_specs=[SMEM, SMEM] + [VMEM] * 6, out...  4.87 us
    ppermute x1, starting transfers between devices, swap_columns(): east = lax.ppermute(for_west, 'tile', west_going)  4.82 us
    unnamed x30, local copies, waits for them, and re-layouts  4.3 us
  transfers between devices with their start and end apart: 8, of which 3 were waited for; matrix products, arithmetic and copies ran while one was open for 0% of the time, Pallas kernels for 27%

profile of v1, /device:TPU:1, one launch (start us, length us, event | category | flops | bytes accessed | tf_op | source)
XLA Modules:
  0.0 91.1 jit_solution(13466468470167674291)
XLA Ops:
  0.6 0.0 copy-start.13
  0.6 0.0 copy-start.1
  0.7 0.0 copy-start.2
  0.7 1.6 %edge_rows.1 = (f32[150,2,128]{2,1,0:T(2,128)S(1)}, f32[150,2,128]{2,1,0:T(2,128)S(1)}) custom-call(f32[75,64,128]{2,1,0:T(8,128)} %x_ref.4, f32[75,64,128]{2,1,0:T(8,128)} %x_ref.5, s32[64,128]{1,0:T(8,128)} %mask_ref.7), custom_call_target="tpu_custom_call" | custom-call | tf_op jit(solution)/shard_map/edge_rows/pallas_call | solution.py:340
  2.3 4.7 %collective-permute-start = (f32[150,2,128]{2,1,0:T(2,128)S(1)}, f32[150,2,128]{2,1,0:T(2,128)S(1)}, u32[]{:S(2)}, u32[]{:S(2)}) collective-permute-start(f32[150,2,128]{2,1,0:T(2,128)S(1)} %get-tuple-element.27), channel_id=1, source_target_pairs={{0,16},{16,32},{32,48},{48,64},{64,80},{80,96},{96,112},{1,17},{17... | collective-permute-start | bytes 460808 | tf_op jit(solution)/shard_map/ppermute | solution.py:736
  7.0 1.9 %collective-permute-start.1 = (f32[150,2,128]{2,1,0:T(2,128)S(1)}, f32[150,2,128]{2,1,0:T(2,128)S(1)}, u32[]{:S(2)}, u32[]{:S(2)}) collective-permute-start(f32[150,2,128]{2,1,0:T(2,128)S(1)} %get-tuple-element.28), channel_id=1, source_target_pairs={{16,0},{32,16},{48,32},{64,48},{80,64},{96,80},{112,96},{17,1},{33... | collective-permute-start | bytes 460808 | tf_op jit(solution)/shard_map/ppermute | solution.py:737
  8.9 0.0 copy-done.13
  8.9 0.0 copy-start.6
  9.0 1.2 %copy-done.6 = bf16[63,8192]{1,0:T(8,128)(2,1)S(1)} copy-done((bf16[63,8192]{1,0:T(8,128)(2,1)S(1)}, bf16[63,8192]{1,0:T(8,128)(2,1)}, u32[]{:S(2)}) %copy-start.6) | copy-done | bytes 1032216
  10.2 1.6 %copy-done.8 = f32[64,8192]{1,0:T(8,128)S(1)} copy-done((f32[64,8192]{1,0:T(8,128)S(1)}, f32[64,8192]{1,0:T(8,128)}, u32[]{:S(2)}) %copy-start.8) | copy-done | bytes 2097176
  11.8 2.9 %surface_flux.1.pair_ref = f32[512,128]{1,0:T(8,128)S(1)} custom-call(f32[4,64]{1,0:T(4,128)S(1)} %copy-done.13, f32[64,8192]{1,0:T(8,128)S(1)} %copy-done.8, bf16[63,8192]{1,0:T(8,128)(2,1)S(1)} %copy-done.6), custom_call_target="tpu_custom_call" | custom-call | tf_op jit(solution)/shard_map/surface_flux/pallas_call | solution.py:136
  14.7 0.0 copy-start.11
  14.7 0.0 copy-start.14
  14.7 0.0 collective-permute-done.north_ref
  14.7 0.0 collective-permute-done.1.south_ref
  14.7 0.0 copy-done.1
  14.7 0.0 copy-done.2
  14.7 0.0 copy-done.9
  14.7 1.9 %pack_columns.1 = (f32[2,3,72,128]{3,2,1,0:T(8,128)S(1)}, f32[3,72,128]{2,1,0:T(8,128)S(1)}, f32[3,72,128]{2,1,0:T(8,128)S(1)}) custom-call(f32[75,64,128]{2,1,0:T(8,128)S(1)} %copy-done.2, f32[75,64,128]{2,1,0:T(8,128)S(1)} %copy-done.1, s32[64,128]{1,0:T(8,128)S(1)} %copy-done.9, f32[150,2,128]{2,1,0:T(2,128)S(1)} %collective-permute-done.north_ref, ...), custom_call_target="tpu_custom_call" | custom-call | tf_op jit(solution)/shard_map/pack_columns/pallas_call | solution.py:395
  16.6 1.3 %collective-permute-start.2 = (f32[3,72,128]{2,1,0:T(8,128)S(1)}, f32[3,72,128]{2,1,0:T(8,128)S(1)}, u32[]{:S(2)}, u32[]{:S(2)}) collective-permute-start(f32[3,72,128]{2,1,0:T(8,128)S(1)} %get-tuple-element.37), channel_id=1, source_target_pairs={{0,1},{1,2},{2,3},{3,4},{4,5},{5,6},{6,7},{7,8},{8,9},{9,10},{10,1... | collective-permute-start | bytes 331784 | tf_op jit(solution)/shard_map/ppermute | solution.py:745
  17.9 4.8 %collective-permute-start.3 = (f32[3,72,128]{2,1,0:T(8,128)S(1)}, f32[3,72,128]{2,1,0:T(8,128)S(1)}, u32[]{:S(2)}, u32[]{:S(2)}) collective-permute-start(f32[3,72,128]{2,1,0:T(8,128)S(1)} %get-tuple-element.38), channel_id=1, source_target_pairs={{1,0},{2,1},{3,2},{4,3},{5,4},{6,5},{7,6},{8,7},{9,8},{10,9},{11,1... | collective-permute-start | bytes 331784 | tf_op jit(solution)/shard_map/ppermute | solution.py:746
  22.7 0.0 copy-start.12
  22.7 4.2 %remap.1 = (f32[2176,128]{1,0:T(8,128)}, s32[256]{0:T(256)S(1)}) custom-call(s32[4,64]{1,0:T(4,128)S(1)} %bitcast.15, s32[4,64]{1,0:T(4,128)S(1)} %bitcast.16, s32[4,64]{1,0:T(4,128)S(1)} %bitcast.17, f32[512,128]{1,0:T(8,128)S(1)} %surface_flux.1.pair_ref, bf16[256,128,128]{2,1,0:T(8,128)(2,1)S(1)} %copy-done), custom_call_target="tpu_custom_call" | custom-call | tf_op jit(solution)/shard_map/remap/pallas_call | solution.py:231
  26.9 0.0 collective-permute-done.2.west_ref
  26.9 0.0 collective-permute-done.3.east_ref
  26.9 8.7 %all-to-all-start = ((f32[128,1,2176]{2,1,0:T(1,128)}), f32[128,1,2176]{2,1,0:T(1,128)}, u32[]{:S(2)}, u32[]{:S(2)}) async-start(f32[128,1,2176]{2,1,0:T(1,128)} %bitcast.18), calls=%async_computation | async-start | bytes 2228224 | tf_op jit(solution)/shard_map/all_to_all | solution.py:751
  35.6 0.1 add_convert_fusion.ends_ref
  35.7 0.0 copy-done.10
  35.7 5.1 %ocean_tangent.1.x_ref = f32[75,64,128]{2,1,0:T(8,128)S(1)} custom-call(f32[74]{0:T(128)S(1)} %copy-done.12, s32[2]{0:T(128)S(1)} %add_convert_fusion.ends_ref, f32[4,75]{1,0:T(4,128)S(1)} %bitcast.12, f32[75,64,128]{2,1,0:T(8,128)S(1)} %copy-done.1, s32[64,128]{1,0:T(8,128)S(1)} %copy-done.9, f32[150,2,128]{2,1,0:T(2,128)S(1)} %collective-permute-done.north_ref, ...), custom_call_target="tpu_custom_call" | custom-call | tf_op jit(solution)/shard_map/ocean_tangent/pallas_call | solution.py:558
  40.8 0.0 copy-start.4
  40.8 1.4 %copy-done.4 = f32[75,64,128]{2,1,0:T(8,128)} copy-done((f32[75,64,128]{2,1,0:T(8,128)}, f32[75,64,128]{2,1,0:T(8,128)S(1)}, u32[]{:S(2)}) %copy-start.4) | copy-done | bytes 2457624
  42.2 0.0 copy-done.3
  42.2 6.2 %ocean_adjoint.1 = (f32[75,64,128]{2,1,0:T(8,128)}, f32[64,512]{1,0:T(8,128)S(1)}) custom-call(f32[74]{0:T(128)S(1)} %copy-done.12, s32[2]{0:T(128)S(1)} %add_convert_fusion.ends_ref, f32[4,75]{1,0:T(4,128)S(1)} %bitcast.13, f32[75,64,128]{2,1,0:T(8,128)S(1)} %copy-done.3, s32[64,128]{1,0:T(8,128)S(1)} %copy-done.9, ...), custom_call_target="tpu_custom_call" | custom-call | tf_op jit(solution)/shard_map/ocean_adjoint/pallas_call | solution.py:558
  48.5 6.5 %all-to-all-done = f32[128,1,2176]{2,1,0:T(1,128)} async-done(((f32[128,1,2176]{2,1,0:T(1,128)}), f32[128,1,2176]{2,1,0:T(1,128)}, u32[]{:S(2)}, u32[]{:S(2)}) %all-to-all-start) | async-done | bytes 1114144 | tf_op jit(solution)/shard_map/all_to_all | solution.py:751
  54.9 2.9 %answer.1 = f32[2048,128]{1,0:T(8,128)} custom-call(f32[2176,128]{1,0:T(8,128)} %bitcast.6.msg_ref, f32[64,512]{1,0:T(8,128)S(1)} %get-tuple-element.50.flux_ref), custom_call_target="tpu_custom_call" | custom-call | tf_op jit(solution)/shard_map/answer/pallas_call | solution.py:600
  57.8 5.6 %all-to-all-start.1 = ((f32[128,4,4,128]{3,2,1,0:T(4,128)}), f32[128,4,4,128]{3,2,1,0:T(4,128)}, u32[]{:S(2)}, u32[]{:S(2)}) async-start(f32[128,4,4,128]{3,2,1,0:T(4,128)} %bitcast.7), calls=%async_computation.1 | async-start | bytes 2097152 | tf_op jit(solution)/shard_map/all_to_all | solution.py:751
  63.5 0.1 subtract_multiply_fusion.1
  63.6 0.1 broadcast_multiply_fusion.1
  63.6 0.1 subtract_multiply_fusion
  63.7 0.1 pad_subtract_fusion
  63.8 1.7 %collect.1 = (f32[4,64,128]{2,1,0:T(8,128)S(1)}, f32[64,128]{1,0:T(8,128)S(1)}, f32[5,2,128]{2,1,0:T(2,128)S(1)}, f32[5,2,128]{2,1,0:T(2,128)S(1)}) custom-call(f32[2176,128]{1,0:T(8,128)} %bitcast.6.msg_ref), custom_call_target="tpu_custom_call" | custom-call | tf_op jit(solution)/shard_map/collect/pallas_call | solution.py:647
  65.5 3.6 %collective-permute-start.4 = (f32[5,2,128]{2,1,0:T(2,128)S(1)}, f32[5,2,128]{2,1,0:T(2,128)S(1)}, u32[]{:S(2)}, u32[]{:S(2)}) collective-permute-start(f32[5,2,128]{2,1,0:T(2,128)S(1)} %get-tuple-element.46), channel_id=1, source_target_pairs={{0,16},{16,32},{32,48},{48,64},{64,80},{80,96},{96,112},{1,17},{17... | collective-permute-start | bytes 15368 | tf_op jit(solution)/shard_map/ppermute | solution.py:736
  69.1 1.9 %collective-permute-start.5 = (f32[5,2,128]{2,1,0:T(2,128)S(1)}, f32[5,2,128]{2,1,0:T(2,128)S(1)}, u32[]{:S(2)}, u32[]{:S(2)}) collective-permute-start(f32[5,2,128]{2,1,0:T(2,128)S(1)} %get-tuple-element.47), channel_id=1, source_target_pairs={{16,0},{32,16},{48,32},{64,48},{80,64},{96,80},{112,96},{17,1},{33... | collective-permute-start | bytes 15368 | tf_op jit(solution)/shard_map/ppermute | solution.py:737
  71.1 0.0 collective-permute-done.4.north_ref
  71.1 3.5 %collective-permute-done.5.south_ref = f32[5,2,128]{2,1,0:T(2,128)S(1)} collective-permute-done((f32[5,2,128]{2,1,0:T(2,128)S(1)}, f32[5,2,128]{2,1,0:T(2,128)S(1)}, u32[]{:S(2)}, u32[]{:S(2)}) %collective-permute-start.5) | collective-permute-done | bytes 5152 | tf_op jit(solution)/shard_map/ppermute | solution.py:737
  74.5 4.9 %apply_flux.1 = f32[75,64,128]{2,1,0:T(8,128)} custom-call(f32[12,75]{1,0:T(8,128)S(1)} %pad_maximum_fusion.coef_ref, s32[2]{0:T(128)S(1)} %add_convert_fusion.ends_ref, f32[75,64,128]{2,1,0:T(8,128)S(1)} %copy-done.5, s32[64,128]{1,0:T(8,128)S(1)} %copy-done.9, f32[4,64,128]{2,1,0:T(8,128)S(1)} %get-tuple-element.44.flux_ref, ...), custom_call_target="tpu_custom_call" | custom-call | tf_op jit(solution)/shard_map/apply_flux/pallas_call | solution.py:717
  79.4 3.2 %all-to-all-done.1 = f32[128,4,4,128]{3,2,1,0:T(4,128)} async-done(((f32[128,4,4,128]{3,2,1,0:T(4,128)}), f32[128,4,4,128]{3,2,1,0:T(4,128)}, u32[]{:S(2)}, u32[]{:S(2)}) %all-to-all-start.1) | async-done | bytes 1048608 | tf_op jit(solution)/shard_map/all_to_all | solution.py:751
  82.6 8.5 %atm_adjoint.1 = f32[64,8192]{1,0:T(8,128)} custom-call(s32[256]{0:T(256)S(1)} %get-tuple-element.49.slot_ref, f32[4,64]{1,0:T(4,128)S(1)} %copy-done.13, f32[512,4,128]{2,1,0:T(4,128)} %bitcast.8.back_ref, bf16[63,8192]{1,0:T(8,128)(2,1)S(1)} %copy-done.7, bf16[256,128,128]{2,1,0:T(8,128)(2,1)} %w_hbm.1), custom_call_target="tpu_custom_call" | custom-call | tf_op jit(solution)/shard_map/atm_adjoint/pallas_call | solution.py:302
  (14 shorter events, 0.0 us)
Async XLA Ops:
  0.6 8.3 %copy-start.13 = (f32[4,64]{1,0:T(4,128)S(1)}, f32[4,64]{1,0:T(4,128)}, u32[]{:S(2)}) copy-start(f32[4,64]{1,0:T(4,128)} %coef_ref.3) | copy-start | bytes 3076
  0.6 14.1 %copy-start.1 = (f32[75,64,128]{2,1,0:T(8,128)S(1)}, f32[75,64,128]{2,1,0:T(8,128)}, u32[]{:S(2)}) copy-start(f32[75,64,128]{2,1,0:T(8,128)} %x_ref.5) | copy-start | bytes 7372804
  0.7 14.1 %copy-start.2 = (f32[75,64,128]{2,1,0:T(8,128)S(1)}, f32[75,64,128]{2,1,0:T(8,128)}, u32[]{:S(2)}) copy-start(f32[75,64,128]{2,1,0:T(8,128)} %x_ref.4) | copy-start | bytes 7372804
  0.7 14.1 %copy-start.9 = (s32[64,128]{1,0:T(8,128)S(1)}, s32[64,128]{1,0:T(8,128)}, u32[]{:S(2)}) copy-start(s32[64,128]{1,0:T(8,128)} %mask_ref.7) | copy-start | bytes 98308
  2.3 12.4 %collective-permute-start = (f32[150,2,128]{2,1,0:T(2,128)S(1)}, f32[150,2,128]{2,1,0:T(2,128)S(1)}, u32[]{:S(2)}, u32[]{:S(2)}) collective-permute-start(f32[150,2,128]{2,1,0:T(2,128)S(1)} %get-tuple-element.27), channel_id=1, source_target_pairs={{0,16},{16,32},{32,48},{48,64},{64,80},{80,96},{96,112},{1,17},{17... | collective-permute-start | bytes 460808 | tf_op jit(solution)/shard_map/ppermute | solution.py:736
  7.0 7.7 %collective-permute-start.1 = (f32[150,2,128]{2,1,0:T(2,128)S(1)}, f32[150,2,128]{2,1,0:T(2,128)S(1)}, u32[]{:S(2)}, u32[]{:S(2)}) collective-permute-start(f32[150,2,128]{2,1,0:T(2,128)S(1)} %get-tuple-element.28), channel_id=1, source_target_pairs={{16,0},{32,16},{48,32},{64,48},{80,64},{96,80},{112,96},{17,1},{33... | collective-permute-start | bytes 460808 | tf_op jit(solution)/shard_map/ppermute | solution.py:737
  8.9 1.2 %copy-start.6 = (bf16[63,8192]{1,0:T(8,128)(2,1)S(1)}, bf16[63,8192]{1,0:T(8,128)(2,1)}, u32[]{:S(2)}) copy-start(bf16[63,8192]{1,0:T(8,128)(2,1)} %mix_ref.3) | copy-start | bytes 3096580
  10.2 1.6 %copy-start.8 = (f32[64,8192]{1,0:T(8,128)S(1)}, f32[64,8192]{1,0:T(8,128)}, u32[]{:S(2)}) copy-start(f32[64,8192]{1,0:T(8,128)} %x_ref.3) | copy-start | bytes 6291460
  11.8 11.0 %copy-start = (bf16[256,128,128]{2,1,0:T(8,128)(2,1)S(1)}, bf16[256,128,128]{2,1,0:T(8,128)(2,1)}, u32[]{:S(2)}) copy-start(bf16[256,128,128]{2,1,0:T(8,128)(2,1)} %w_hbm.1) | copy-start | bytes 25165828
  14.7 8.0 %copy-start.11 = (s32[64,4]{0,1:T(4,128)S(1)}, s32[64,4]{0,1:T(4,128)}, u32[]{:S(2)}) copy-start(s32[64,4]{0,1:T(4,128)} %param.15) | copy-start | bytes 3076
  14.7 8.0 %copy-start.14 = (s32[64,4]{0,1:T(4,128)S(1)}, s32[64,4]{0,1:T(4,128)}, u32[]{:S(2)}) copy-start(s32[64,4]{0,1:T(4,128)} %param.16) | copy-start | bytes 3076
  16.6 10.3 %collective-permute-start.2 = (f32[3,72,128]{2,1,0:T(8,128)S(1)}, f32[3,72,128]{2,1,0:T(8,128)S(1)}, u32[]{:S(2)}, u32[]{:S(2)}) collective-permute-start(f32[3,72,128]{2,1,0:T(8,128)S(1)} %get-tuple-element.37), channel_id=1, source_target_pairs={{0,1},{1,2},{2,3},{3,4},{4,5},{5,6},{6,7},{7,8},{8,9},{9,10},{10,1... | collective-permute-start | bytes 331784 | tf_op jit(solution)/shard_map/ppermute | solution.py:745
  17.9 9.0 %collective-permute-start.3 = (f32[3,72,128]{2,1,0:T(8,128)S(1)}, f32[3,72,128]{2,1,0:T(8,128)S(1)}, u32[]{:S(2)}, u32[]{:S(2)}) collective-permute-start(f32[3,72,128]{2,1,0:T(8,128)S(1)} %get-tuple-element.38), channel_id=1, source_target_pairs={{1,0},{2,1},{3,2},{4,3},{5,4},{6,5},{7,6},{8,7},{9,8},{10,9},{11,1... | collective-permute-start | bytes 331784 | tf_op jit(solution)/shard_map/ppermute | solution.py:746
  22.7 13.0 %copy-start.10 = (f32[75,4]{0,1:T(4,128)S(1)}, f32[75,4]{0,1:T(4,128)}, u32[]{:S(2)}) copy-start(f32[75,4]{0,1:T(4,128)} %param.19) | copy-start | bytes 3604
  22.7 13.0 %copy-start.12 = (f32[74]{0:T(128)S(1)}, f32[74]{0:T(128)}, u32[]{:S(2)}) copy-start(f32[74]{0:T(128)} %k_ref.3) | copy-start | bytes 892
  26.9 28.0 %all-to-all-start = ((f32[128,1,2176]{2,1,0:T(1,128)}), f32[128,1,2176]{2,1,0:T(1,128)}, u32[]{:S(2)}, u32[]{:S(2)}) async-start(f32[128,1,2176]{2,1,0:T(1,128)} %bitcast.18), calls=%async_computation | async-start | bytes 2228224 | tf_op jit(solution)/shard_map/all_to_all | solution.py:751
  35.7 6.5 %copy-start.3 = (f32[75,64,128]{2,1,0:T(8,128)S(1)}, f32[75,64,128]{2,1,0:T(8,128)}, u32[]{:S(2)}) copy-start(f32[75,64,128]{2,1,0:T(8,128)} %x_ref.4) | copy-start | bytes 7372804
  40.8 1.4 %copy-start.4 = (f32[75,64,128]{2,1,0:T(8,128)}, f32[75,64,128]{2,1,0:T(8,128)S(1)}, u32[]{:S(2)}) copy-start(f32[75,64,128]{2,1,0:T(8,128)S(1)} %ocean_tangent.1.x_ref) | copy-start | bytes 7372804
  54.9 19.6 %copy-start.5 = (f32[75,64,128]{2,1,0:T(8,128)S(1)}, f32[75,64,128]{2,1,0:T(8,128)}, u32[]{:S(2)}) copy-start(f32[75,64,128]{2,1,0:T(8,128)} %copy-done.4) | copy-start | bytes 7372804
  57.8 24.7 %all-to-all-start.1 = ((f32[128,4,4,128]{3,2,1,0:T(4,128)}), f32[128,4,4,128]{3,2,1,0:T(4,128)}, u32[]{:S(2)}, u32[]{:S(2)}) async-start(f32[128,4,4,128]{3,2,1,0:T(4,128)} %bitcast.7), calls=%async_computation.1 | async-start | bytes 2097152 | tf_op jit(solution)/shard_map/all_to_all | solution.py:751
  65.5 5.6 %collective-permute-start.4 = (f32[5,2,128]{2,1,0:T(2,128)S(1)}, f32[5,2,128]{2,1,0:T(2,128)S(1)}, u32[]{:S(2)}, u32[]{:S(2)}) collective-permute-start(f32[5,2,128]{2,1,0:T(2,128)S(1)} %get-tuple-element.46), channel_id=1, source_target_pairs={{0,16},{16,32},{32,48},{48,64},{64,80},{80,96},{96,112},{1,17},{17... | collective-permute-start | bytes 15368 | tf_op jit(solution)/shard_map/ppermute | solution.py:736
  69.1 5.4 %collective-permute-start.5 = (f32[5,2,128]{2,1,0:T(2,128)S(1)}, f32[5,2,128]{2,1,0:T(2,128)S(1)}, u32[]{:S(2)}, u32[]{:S(2)}) collective-permute-start(f32[5,2,128]{2,1,0:T(2,128)S(1)} %get-tuple-element.47), channel_id=1, source_target_pairs={{16,0},{32,16},{48,32},{64,48},{80,64},{96,80},{112,96},{17,1},{33... | collective-permute-start | bytes 15368 | tf_op jit(solution)/shard_map/ppermute | solution.py:737
  74.5 8.0 %copy-start.7 = (bf16[63,8192]{1,0:T(8,128)(2,1)S(1)}, bf16[63,8192]{1,0:T(8,128)(2,1)}, u32[]{:S(2)}) copy-start(bf16[63,8192]{1,0:T(8,128)(2,1)} %mix_ref.3) | copy-start | bytes 3096580

commit v2 on v1

--- a/solution.py
+++ b/solution.py
@@ -41,6 +41,12 @@
     return pltpu.CompilerParams(vmem_limit_bytes=mib * MIB)
 
 
+def cost(us):
+    return pl.CostEstimate(
+        flops=int(us * 300000000), bytes_accessed=int(us * 900000), transcendentals=0
+    )
+
+
 def in_hbm(v):
     return pltpu.with_memory_space_constraint(v, pltpu.HBM)
 
@@ -106,8 +112,22 @@
     )
 
 
-def surface_flux_kernel(coef_ref, x_ref, mix_ref, out_ref, xs, ms):
-    def work(step, carry):
+def surface_flux_kernel(coef_ref, x_hbm, mix_hbm, out_ref, x_ref, mix_ref, xs, ms, sems):
+    cols = GRP * B
+
+    def x_copy(s):
+        part = pl.ds(s * cols, cols)
+        return pltpu.make_async_copy(x_hbm.at[:, part], x_ref.at[:, part], sems.at[0, s])
+
+    def mix_copy(s):
+        part = pl.ds(s * cols, cols)
+        return pltpu.make_async_copy(mix_hbm.at[:, part], mix_ref.at[:, part], sems.at[1, s])
+
+    for s in range(STEPS):
+        x_copy(s).start()
+        mix_copy(s).start()
+
+    def one(step):
         for b in range(GRP):
             at = block_lanes(step * GRP + b)
             xs[step % 2, pl.ds(b * PITCH, LA), :] = x_ref[:, at]
@@ -127,21 +147,34 @@
             at = step * GRP * 2 * FLD + f
             out_ref[pl.ds(at, GRP, stride=2 * FLD), :] = high
             out_ref[pl.ds(at + FLD, GRP, stride=2 * FLD), :] = sums[f] - high
+
+    def work(pair, carry):
+        for half in range(2):
+            x_copy(2 * pair + half).wait()
+            mix_copy(2 * pair + half).wait()
+        for half in range(2):
+            one(2 * pair + half)
         return carry
 
-    lax.fori_loop(0, STEPS, work, 0, unroll=2)
+    lax.fori_loop(0, STEPS // 2, work, 0)
 
 
 def surface_flux(coef, x, mix):
     return pl.pallas_call(
         surface_flux_kernel,
-        in_specs=[SMEM, VMEM, VMEM],
+        in_specs=[SMEM, ANY, ANY],
         out_specs=VMEM,
         out_shape=f32(NBA * 2 * FLD, B),
-        scratch_shapes=[pltpu.VMEM((2, GRP * PITCH, B), F32), pltpu.VMEM((2, GRP * PITCH, B), F32)],
+        scratch_shapes=[
+            pltpu.VMEM((LA, NBA * B), F32),
+            pltpu.VMEM((LA - 1, NBA * B), BF16),
+            pltpu.VMEM((2, GRP * PITCH, B), F32),
+            pltpu.VMEM((2, GRP * PITCH, B), F32),
+            pltpu.SemaphoreType.DMA((2, STEPS)),
+        ],
         compiler_params=params(12),
         name="surface_flux",
-    )(coef, x, mix)
+    )(coef, in_hbm(x), in_hbm(mix))
 
 
 def columns_of(rows):
@@ -255,8 +288,7 @@
     for s in range(STEPS):
         w_copy(s).start()
 
-    def work(step, carry):
-        w_copy(step).wait()
+    def one(step):
         for i in range(0, GRP, 2):
             row = step * GRP + i
             total = None
@@ -290,10 +322,17 @@
         sweep_levels(load, lambda l: level_rows(ms, l), emit)
         for b in range(GRP):
             out_ref[:, block_lanes(step * GRP + b)] = steps_ref[pl.ds(b * PITCH, LA), :]
-        out_copy(step).start()
+
+    def work(pair, carry):
+        for half in range(2):
+            w_copy(2 * pair + half).wait()
+        for half in range(2):
+            one(2 * pair + half)
+        for half in range(2):
+            out_copy(2 * pair + half).start()
         return carry
 
-    lax.fori_loop(0, STEPS, work, 0, unroll=2)
+    lax.fori_loop(0, STEPS // 2, work, 0)
     for s in range(STEPS):
         out_copy(s).wait()
 
@@ -310,7 +349,7 @@
             pltpu.VMEM((GRP * FLD, B), F32),
             pltpu.VMEM((GRP * PITCH, B), F32),
             pltpu.VMEM((LA, NBA * B), F32),
-            pltpu.SemaphoreType.DMA((2, STEPS)),
+            pltpu.SemaphoreType.DMA((3, STEPS)),
         ],
         compiler_params=params(24),
         name="atm_adjoint",
@@ -493,6 +532,10 @@
     wide = lanes(OY)
     edge_lane = (wide < 2) | (wide >= B - 2)
 
+    def out_copy(group):
+        part = pl.ds(group * LEVELS, LEVELS)
+        return pltpu.make_async_copy(out_ref.at[part], out_hbm.at[part], sem.at[group])
+
     def step(src, start, count, second):
         rows = pl.ds(start, count)
 
@@ -520,14 +563,14 @@
                 else:
                     first[level, rows, :] = done * keep
                 below = flow
+            if second:
+                out_copy(group).start()
             return below
 
         lax.fori_loop(0, LO // LEVELS, body, jnp.zeros((count, B), F32))
 
     step(state, 8, OY + 16, False)
     step(first, TOP, OY, True)
-    out_copy = pltpu.make_async_copy(out_ref, out_hbm, sem.at[0])
-    out_copy.start()
 
     if adjoint:
         tall = 32
@@ -543,14 +586,15 @@
             )
             for f in range(FLD):
                 flux_ref[rows, f * B : (f + 1) * B] = sums[f]
-    out_copy.wait()
+    for group in range(LO // LEVELS):
+        out_copy(group).wait()
 
 
 def ocean_steps(adjoint, k, ends, pen, x, mask, north, south, own, west, east):
     at = 0 if adjoint else 1
     rim = pl.BlockSpec((LO, 2, B), lambda i: (at, 0, 0))
     full = lambda *shape: pl.BlockSpec(shape, lambda i: (0,) * len(shape))
-    shapes = [f32(LO, OY, B)]
+    shapes = [pltpu.HBM((LO, OY, B), F32)]
     outs = [ANY]
     if adjoint:
         shapes.append(f32(OY, FLD * B))
@@ -577,30 +621,47 @@
             pltpu.VMEM((LO + 1, TALL, B), F32),
             pltpu.VMEM((PLANES, OY, B), F32),
             pltpu.VMEM((LO, OY, B), F32),
-            pltpu.SemaphoreType.DMA((1,)),
+            pltpu.SemaphoreType.DMA((LO // LEVELS,)),
         ],
         compiler_params=params(24),
+        cost_estimate=cost(6),
         name="ocean_adjoint" if adjoint else "ocean_tangent",
     )(k, ends, pen, x, mask, north, south, own, west, east)
 
 
-def answer_kernel(msg_ref, flux_ref, out_ref):
-    labels = msg_ref[pl.ds(MSG - 1, DEV, stride=MSG), :]
+def answer_kernel(msg_ref, flux_ref, out_hbm, out_ref, sems):
+    quarter = DEV // 4
     gh, gl = split2(flux_ref[...])
     table = jnp.concatenate([gh, gl], axis=0)
-    want = lax.broadcasted_iota(jnp.int32, (DEV, B), 1) % OY + 1
-    for c in range(CAP):
-        pick = (labels[:, c : c + 1].astype(jnp.int32) == want).astype(F32).astype(BF16)
+    want = lax.broadcasted_iota(jnp.int32, (quarter, B), 1) % OY + 1
+    size = quarter * CAP * FLD
+    copies = []
+    for q in range(4):
+        labels = msg_ref[pl.ds(q * quarter * MSG + MSG - 1, quarter, stride=MSG), :].astype(jnp.int32)
+        pick = jnp.concatenate(
+            [(labels[:, c : c + 1] == want).astype(F32) for c in range(CAP)], axis=0
+        ).astype(BF16)
         rows = dot(pick, table)
-        for f in range(FLD):
-            out_ref[pl.ds(c * FLD + f, DEV, stride=CAP * FLD), :] = rows[:, f * B : (f + 1) * B]
+        for c in range(CAP):
+            for f in range(FLD):
+                at = pl.ds(q * size + c * FLD + f, quarter, stride=CAP * FLD)
+                out_ref[at, :] = rows[c * quarter : (c + 1) * quarter, f * B : (f + 1) * B]
+        part = pl.ds(q * size, size)
+        copies.append(pltpu.make_async_copy(out_ref.at[part], out_hbm.at[part], sems.at[q]))
+        copies[-1].start()
+    for c in copies:
+        c.wait()
 
 
 def answer(msg, flux):
     return pl.pallas_call(
         answer_kernel,
-        out_shape=f32(DEV * CAP * FLD, B),
+        in_specs=[VMEM, VMEM],
+        out_specs=ANY,
+        out_shape=pltpu.HBM((DEV * CAP * FLD, B), F32),
+        scratch_shapes=[pltpu.VMEM((DEV * CAP * FLD, B), F32), pltpu.SemaphoreType.DMA((4,))],
         compiler_params=params(12),
+        cost_estimate=cost(2.5),
         name="answer",
     )(msg, flux)
 
@@ -648,6 +709,7 @@
         collect_kernel,
         out_shape=[f32(FLD, OY, B), f32(OY, B), f32(FLD + 1, 2, B), f32(FLD + 1, 2, B)],
         compiler_params=params(12),
+        cost_estimate=cost(1.6),
         name="collect",
     )(msg)
 

time: 91.5 us -> 87.6 us (0.957)
  local copies, waits for them, and re-layouts: 4.3 us -> 1.75 us
  starting transfers between devices: 32.6 us -> 31.5 us
  waiting for transfers between devices: 13.1 us -> 12 us
    unnamed x30 -> x24, local copies, waits for them, and re-layouts: 4.3 us -> 1.75 us
    pallas_call x1, Pallas kernels: 8.51 us -> 6.9 us  [atm_adjoint(): pl.pallas_call(atm_adjoint_kernel, in_specs=[SMEM, SMEM, VMEM, VMEM, ANY]...]
    pallas_call x2, Pallas kernels: 11.3 us -> 12.5 us  [ocean_steps(): pl.pallas_call(functools.partial(ocean_kernel, adjoint), grid=(1,), in_sp...]
    pallas_call x2, Pallas kernels: 5.81 us -> 6.96 us  [the longest x1 4.42 us: surface_flux(): pl.pallas_call(surface_flux_kernel, in_specs=[SMEM, ANY, ANY], out_specs=...]
    all_to_all x2, starting transfers between devices: 14.3 us -> 13.2 us  [exchange(): lax.all_to_all(rows, ('face', 'tile'), split_axis=0, concat_axis=0, tiled...]
    all_to_all x2, waiting for transfers between devices: 9.62 us -> 8.55 us  [exchange(): lax.all_to_all(rows, ('face', 'tile'), split_axis=0, concat_axis=0, tiled...]
  transfers between devices with their start and end apart: 8 -> 8, of which waited for: 3 -> 4; matrix products, arithmetic and copies ran while one was open for 0% -> 0% of each run, Pallas kernels for 27% -> 32%
where the time goes in v2:
time: 87.6 us; the launch traced here: 87.2 us
  Pallas kernels  40.6 us (46%)
  starting transfers between devices  31.5 us (36%)
  waiting for transfers between devices  12 us (14%)
  local copies, waits for them, and re-layouts  1.75 us (2%)
  between operations  0.89 us (1%)
    all_to_all x2, starting transfers between devices, exchange(): lax.all_to_all(rows, ('face', 'tile'), split_axis=0, concat_axis=0, tiled...  13.2 us
    pallas_call x2, Pallas kernels, ocean_steps(): pl.pallas_call(functools.partial(ocean_kernel, adjoint), grid=(1,), in_sp...  12.5 us
    all_to_all x2, waiting for transfers between devices, exchange(): lax.all_to_all(rows, ('face', 'tile'), split_axis=0, concat_axis=0, tiled...  8.55 us
    ppermute x2, starting transfers between devices, swap_rows(): north = lax.ppermute(high_rows, 'face', south_going)  8.32 us
    pallas_call x1, Pallas kernels, atm_adjoint(): pl.pallas_call(atm_adjoint_kernel, in_specs=[SMEM, SMEM, VMEM, VMEM, ANY]...  6.9 us
    pallas_call x1, Pallas kernels, apply_flux(): pl.pallas_call(apply_flux_kernel, in_specs=[SMEM, SMEM] + [VMEM] * 6, out...  4.98 us
    ppermute x1, starting transfers between devices, swap_columns(): east = lax.ppermute(for_west, 'tile', west_going)  4.82 us
    pallas_call x1, Pallas kernels, surface_flux(): pl.pallas_call(surface_flux_kernel, in_specs=[SMEM, ANY, ANY], out_specs=...  4.42 us
  transfers between devices with their start and end apart: 8, of which 4 were waited for; matrix products, arithmetic and copies ran while one was open for 0% of the time, Pallas kernels for 32%

profile of v2, /device:TPU:1, one launch (start us, length us, event | category | flops | bytes accessed | tf_op | source)
XLA Modules:
  0.0 87.2 jit_solution(7613114473686615402)
XLA Ops:
  0.6 0.0 copy-start.9
  0.6 0.0 copy-start.1
  0.7 0.0 copy-start.2
  0.7 1.6 %edge_rows.1 = (f32[150,2,128]{2,1,0:T(2,128)S(1)}, f32[150,2,128]{2,1,0:T(2,128)S(1)}) custom-call(f32[75,64,128]{2,1,0:T(8,128)} %x_ref.2, f32[75,64,128]{2,1,0:T(8,128)} %x_ref.3, s32[64,128]{1,0:T(8,128)} %mask_ref.7), custom_call_target="tpu_custom_call" | custom-call | tf_op jit(solution)/shard_map/edge_rows/pallas_call | solution.py:379
  2.3 0.0 copy-start.6
  2.3 4.7 %collective-permute-start = (f32[150,2,128]{2,1,0:T(2,128)S(1)}, f32[150,2,128]{2,1,0:T(2,128)S(1)}, u32[]{:S(2)}, u32[]{:S(2)}) collective-permute-start(f32[150,2,128]{2,1,0:T(2,128)S(1)} %get-tuple-element.27), channel_id=1, source_target_pairs={{0,16},{16,32},{32,48},{48,64},{64,80},{80,96},{96,112},{1,17},{17... | collective-permute-start | bytes 460808 | tf_op jit(solution)/shard_map/ppermute | solution.py:798
  7.0 1.9 %collective-permute-start.1 = (f32[150,2,128]{2,1,0:T(2,128)S(1)}, f32[150,2,128]{2,1,0:T(2,128)S(1)}, u32[]{:S(2)}, u32[]{:S(2)}) collective-permute-start(f32[150,2,128]{2,1,0:T(2,128)S(1)} %get-tuple-element.28), channel_id=1, source_target_pairs={{16,0},{32,16},{48,32},{64,48},{80,64},{96,80},{112,96},{17,1},{33... | collective-permute-start | bytes 460808 | tf_op jit(solution)/shard_map/ppermute | solution.py:799
  8.9 0.0 copy-done.9
  8.9 0.0 copy-start
  9.0 4.4 %surface_flux.1.pair_ref = f32[512,128]{1,0:T(8,128)S(1)} custom-call(f32[4,64]{1,0:T(4,128)S(1)} %copy-done.9, f32[64,8192]{1,0:T(8,128)} %x_hbm.1, bf16[63,8192]{1,0:T(8,128)(2,1)} %mix_ref.1), custom_call_target="tpu_custom_call" | custom-call | tf_op jit(solution)/shard_map/surface_flux/pallas_call | solution.py:163
  13.4 0.0 copy-start.8
  13.4 0.0 copy-start.10
  13.4 0.0 collective-permute-done.north_ref
  13.4 0.1 collective-permute-done.1.south_ref
  13.5 0.0 copy-done.1
  13.5 0.0 copy-done.2
  13.5 0.0 copy-done.6
  13.5 1.9 %pack_columns.1 = (f32[2,3,72,128]{3,2,1,0:T(8,128)S(1)}, f32[3,72,128]{2,1,0:T(8,128)S(1)}, f32[3,72,128]{2,1,0:T(8,128)S(1)}) custom-call(f32[75,64,128]{2,1,0:T(8,128)S(1)} %copy-done.2, f32[75,64,128]{2,1,0:T(8,128)S(1)} %copy-done.1, s32[64,128]{1,0:T(8,128)S(1)} %copy-done.6, f32[150,2,128]{2,1,0:T(2,128)S(1)} %collective-permute-done.north_ref, ...), custom_call_target="tpu_custom_call" | custom-call | tf_op jit(solution)/shard_map/pack_columns/pallas_call | solution.py:434
  15.4 1.3 %collective-permute-start.2 = (f32[3,72,128]{2,1,0:T(8,128)S(1)}, f32[3,72,128]{2,1,0:T(8,128)S(1)}, u32[]{:S(2)}, u32[]{:S(2)}) collective-permute-start(f32[3,72,128]{2,1,0:T(8,128)S(1)} %get-tuple-element.37), channel_id=1, source_target_pairs={{0,1},{1,2},{2,3},{3,4},{4,5},{5,6},{6,7},{7,8},{8,9},{9,10},{10,1... | collective-permute-start | bytes 331784 | tf_op jit(solution)/shard_map/ppermute | solution.py:807
  16.7 4.8 %collective-permute-start.3 = (f32[3,72,128]{2,1,0:T(8,128)S(1)}, f32[3,72,128]{2,1,0:T(8,128)S(1)}, u32[]{:S(2)}, u32[]{:S(2)}) collective-permute-start(f32[3,72,128]{2,1,0:T(8,128)S(1)} %get-tuple-element.38), channel_id=1, source_target_pairs={{1,0},{2,1},{3,2},{4,3},{5,4},{6,5},{7,6},{8,7},{9,8},{10,9},{11,1... | collective-permute-start | bytes 331784 | tf_op jit(solution)/shard_map/ppermute | solution.py:808
  21.5 0.0 copy-done
  21.5 0.0 copy-done.8
  21.5 0.0 copy-start.11
  21.6 4.2 %remap.1 = (f32[2176,128]{1,0:T(8,128)}, s32[256]{0:T(256)S(1)}) custom-call(s32[4,64]{1,0:T(4,128)S(1)} %bitcast.16, s32[4,64]{1,0:T(4,128)S(1)} %bitcast.17, s32[4,64]{1,0:T(4,128)S(1)} %bitcast.18, f32[512,128]{1,0:T(8,128)S(1)} %surface_flux.1.pair_ref, bf16[256,128,128]{2,1,0:T(8,128)(2,1)S(1)} %copy-done), custom_call_target="tpu_custom_call" | custom-call | tf_op jit(solution)/shard_map/remap/pallas_call | solution.py:264
  25.7 0.0 collective-permute-done.2.west_ref
  25.7 0.0 collective-permute-done.3.east_ref
  25.7 8.6 %all-to-all-start = ((f32[128,1,2176]{2,1,0:T(1,128)}), f32[128,1,2176]{2,1,0:T(1,128)}, u32[]{:S(2)}, u32[]{:S(2)}) async-start(f32[128,1,2176]{2,1,0:T(1,128)} %bitcast.19), calls=%async_computation | async-start | bytes 2228224 | tf_op jit(solution)/shard_map/all_to_all | solution.py:813
  34.3 0.1 add_convert_fusion.ends_ref
  34.4 0.0 copy-done.11
  34.4 6.2 %ocean_tangent.1.x_ref = f32[75,64,128]{2,1,0:T(8,128)} custom-call(f32[74]{0:T(128)S(1)} %copy-done.11, s32[2]{0:T(128)S(1)} %add_convert_fusion.ends_ref, f32[4,75]{1,0:T(4,128)S(1)} %bitcast.13, f32[75,64,128]{2,1,0:T(8,128)S(1)} %copy-done.1, s32[64,128]{1,0:T(8,128)S(1)} %copy-done.6, f32[150,2,128]{2,1,0:T(2,128)S(1)} %collective-permute-done.north_ref, ...), custom_call_target="tpu_custom_call" | custom-call | flops 1800000000 | bytes 5400000 | tf_op jit(solution)/shard_map/ocean_tangent/pallas_call | solution.py:602
  40.7 6.3 %ocean_adjoint.1 = (f32[75,64,128]{2,1,0:T(8,128)}, f32[64,512]{1,0:T(8,128)S(1)}) custom-call(f32[74]{0:T(128)S(1)} %copy-done.11, s32[2]{0:T(128)S(1)} %add_convert_fusion.ends_ref, f32[4,75]{1,0:T(4,128)S(1)} %bitcast.14, f32[75,64,128]{2,1,0:T(8,128)S(1)} %copy-done.3, s32[64,128]{1,0:T(8,128)S(1)} %copy-done.6, ...), custom_call_target="tpu_custom_call" | custom-call | flops 1800000000 | bytes 5400000 | tf_op jit(solution)/shard_map/ocean_adjoint/pallas_call | solution.py:602
  46.9 6.7 %all-to-all-done = f32[128,1,2176]{2,1,0:T(1,128)} async-done(((f32[128,1,2176]{2,1,0:T(1,128)}), f32[128,1,2176]{2,1,0:T(1,128)}, u32[]{:S(2)}, u32[]{:S(2)}) %all-to-all-start) | async-done | bytes 1114144 | tf_op jit(solution)/shard_map/all_to_all | solution.py:813
  53.7 2.5 %answer.1 = f32[2048,128]{1,0:T(8,128)} custom-call(f32[2176,128]{1,0:T(8,128)} %bitcast.6.msg_ref, f32[64,512]{1,0:T(8,128)S(1)} %get-tuple-element.50.flux_ref), custom_call_target="tpu_custom_call" | custom-call | flops 750000000 | bytes 2250000 | tf_op jit(solution)/shard_map/answer/pallas_call | solution.py:657
  56.2 4.6 %all-to-all-start.1 = ((f32[128,4,4,128]{3,2,1,0:T(4,128)}), f32[128,4,4,128]{3,2,1,0:T(4,128)S(1)}, u32[]{:S(2)}, u32[]{:S(2)}) async-start(f32[128,4,4,128]{3,2,1,0:T(4,128)} %bitcast.20), calls=%async_computation.1 | async-start | bytes 2097152 | tf_op jit(solution)/shard_map/all_to_all | solution.py:813
  60.8 0.1 subtract_multiply_fusion.1
  60.9 0.1 broadcast_multiply_fusion.1
  61.0 0.1 subtract_multiply_fusion
  61.1 0.1 pad_subtract_fusion
  61.1 1.7 %collect.1 = (f32[4,64,128]{2,1,0:T(8,128)S(1)}, f32[64,128]{1,0:T(8,128)S(1)}, f32[5,2,128]{2,1,0:T(2,128)S(1)}, f32[5,2,128]{2,1,0:T(2,128)S(1)}) custom-call(f32[2176,128]{1,0:T(8,128)} %bitcast.6.msg_ref), custom_call_target="tpu_custom_call" | custom-call | flops 480000000 | bytes 1440000 | tf_op jit(solution)/shard_map/collect/pallas_call | solution.py:708
  62.8 3.6 %collective-permute-start.4 = (f32[5,2,128]{2,1,0:T(2,128)S(1)}, f32[5,2,128]{2,1,0:T(2,128)S(1)}, u32[]{:S(2)}, u32[]{:S(2)}) collective-permute-start(f32[5,2,128]{2,1,0:T(2,128)S(1)} %get-tuple-element.46), channel_id=1, source_target_pairs={{0,16},{16,32},{32,48},{48,64},{64,80},{80,96},{96,112},{1,17},{17... | collective-permute-start | bytes 15368 | tf_op jit(solution)/shard_map/ppermute | solution.py:798
  66.4 1.9 %collective-permute-start.5 = (f32[5,2,128]{2,1,0:T(2,128)S(1)}, f32[5,2,128]{2,1,0:T(2,128)S(1)}, u32[]{:S(2)}, u32[]{:S(2)}) collective-permute-start(f32[5,2,128]{2,1,0:T(2,128)S(1)} %get-tuple-element.47), channel_id=1, source_target_pairs={{16,0},{32,16},{48,32},{64,48},{80,64},{96,80},{112,96},{17,1},{33... | collective-permute-start | bytes 15368 | tf_op jit(solution)/shard_map/ppermute | solution.py:799
  68.4 0.0 collective-permute-done.4.north_ref
  68.4 3.3 %collective-permute-done.5.south_ref = f32[5,2,128]{2,1,0:T(2,128)S(1)} collective-permute-done((f32[5,2,128]{2,1,0:T(2,128)S(1)}, f32[5,2,128]{2,1,0:T(2,128)S(1)}, u32[]{:S(2)}, u32[]{:S(2)}) %collective-permute-start.5) | collective-permute-done | bytes 5152 | tf_op jit(solution)/shard_map/ppermute | solution.py:799
  71.7 1.7 %copy-done.5 = f32[75,64,128]{2,1,0:T(8,128)S(1)} copy-done((f32[75,64,128]{2,1,0:T(8,128)S(1)}, f32[75,64,128]{2,1,0:T(8,128)}, u32[]{:S(2)}) %copy-start.5) | copy-done | bytes 2457624
  73.4 5.0 %apply_flux.1 = f32[75,64,128]{2,1,0:T(8,128)} custom-call(f32[12,75]{1,0:T(8,128)S(1)} %pad_maximum_fusion.coef_ref, s32[2]{0:T(128)S(1)} %add_convert_fusion.ends_ref, f32[75,64,128]{2,1,0:T(8,128)S(1)} %copy-done.5, s32[64,128]{1,0:T(8,128)S(1)} %copy-done.6, f32[4,64,128]{2,1,0:T(8,128)S(1)} %get-tuple-element.44.flux_ref, ...), custom_call_target="tpu_custom_call" | custom-call | tf_op jit(solution)/shard_map/apply_flux/pallas_call | solution.py:779
  78.4 1.8 %all-to-all-done.1 = f32[128,4,4,128]{3,2,1,0:T(4,128)S(1)} async-done(((f32[128,4,4,128]{3,2,1,0:T(4,128)}), f32[128,4,4,128]{3,2,1,0:T(4,128)S(1)}, u32[]{:S(2)}, u32[]{:S(2)}) %all-to-all-start.1) | async-done | bytes 1048608 | tf_op jit(solution)/shard_map/all_to_all | solution.py:813
  80.3 0.0 copy-done.4
  80.3 6.9 %atm_adjoint.1 = f32[64,8192]{1,0:T(8,128)} custom-call(s32[256]{0:T(256)S(1)} %get-tuple-element.49.slot_ref, f32[4,64]{1,0:T(4,128)S(1)} %copy-done.9, f32[512,4,128]{2,1,0:T(4,128)S(1)} %bitcast.12, bf16[63,8192]{1,0:T(8,128)(2,1)S(1)} %copy-done.4, bf16[256,128,128]{2,1,0:T(8,128)(2,1)} %w_hbm.1), custom_call_target="tpu_custom_call" | custom-call | tf_op jit(solution)/shard_map/atm_adjoint/pallas_call | solution.py:341
  (8 shorter events, 0.0 us)
Async XLA Ops:
  0.6 8.3 %copy-start.9 = (f32[4,64]{1,0:T(4,128)S(1)}, f32[4,64]{1,0:T(4,128)}, u32[]{:S(2)}) copy-start(f32[4,64]{1,0:T(4,128)} %coef_ref.3) | copy-start | bytes 3076
  0.6 12.9 %copy-start.1 = (f32[75,64,128]{2,1,0:T(8,128)S(1)}, f32[75,64,128]{2,1,0:T(8,128)}, u32[]{:S(2)}) copy-start(f32[75,64,128]{2,1,0:T(8,128)} %x_ref.3) | copy-start | bytes 7372804
  0.7 12.9 %copy-start.2 = (f32[75,64,128]{2,1,0:T(8,128)S(1)}, f32[75,64,128]{2,1,0:T(8,128)}, u32[]{:S(2)}) copy-start(f32[75,64,128]{2,1,0:T(8,128)} %x_ref.2) | copy-start | bytes 7372804
  2.3 11.3 %copy-start.6 = (s32[64,128]{1,0:T(8,128)S(1)}, s32[64,128]{1,0:T(8,128)}, u32[]{:S(2)}) copy-start(s32[64,128]{1,0:T(8,128)} %mask_ref.7) | copy-start | bytes 98308
  2.3 11.1 %collective-permute-start = (f32[150,2,128]{2,1,0:T(2,128)S(1)}, f32[150,2,128]{2,1,0:T(2,128)S(1)}, u32[]{:S(2)}, u32[]{:S(2)}) collective-permute-start(f32[150,2,128]{2,1,0:T(2,128)S(1)} %get-tuple-element.27), channel_id=1, source_target_pairs={{0,16},{16,32},{32,48},{48,64},{64,80},{80,96},{96,112},{1,17},{17... | collective-permute-start | bytes 460808 | tf_op jit(solution)/shard_map/ppermute | solution.py:798
  7.0 6.5 %collective-permute-start.1 = (f32[150,2,128]{2,1,0:T(2,128)S(1)}, f32[150,2,128]{2,1,0:T(2,128)S(1)}, u32[]{:S(2)}, u32[]{:S(2)}) collective-permute-start(f32[150,2,128]{2,1,0:T(2,128)S(1)} %get-tuple-element.28), channel_id=1, source_target_pairs={{16,0},{32,16},{48,32},{64,48},{80,64},{96,80},{112,96},{17,1},{33... | collective-permute-start | bytes 460808 | tf_op jit(solution)/shard_map/ppermute | solution.py:799
  8.9 12.6 %copy-start = (bf16[256,128,128]{2,1,0:T(8,128)(2,1)S(1)}, bf16[256,128,128]{2,1,0:T(8,128)(2,1)}, u32[]{:S(2)}) copy-start(bf16[256,128,128]{2,1,0:T(8,128)(2,1)} %w_hbm.1) | copy-start | bytes 25165828
  13.4 8.2 %copy-start.8 = (s32[64,4]{0,1:T(4,128)S(1)}, s32[64,4]{0,1:T(4,128)}, u32[]{:S(2)}) copy-start(s32[64,4]{0,1:T(4,128)} %param.15) | copy-start | bytes 3076
  13.4 8.1 %copy-start.10 = (s32[64,4]{0,1:T(4,128)S(1)}, s32[64,4]{0,1:T(4,128)}, u32[]{:S(2)}) copy-start(s32[64,4]{0,1:T(4,128)} %param.16) | copy-start | bytes 3076
  15.4 10.3 %collective-permute-start.2 = (f32[3,72,128]{2,1,0:T(8,128)S(1)}, f32[3,72,128]{2,1,0:T(8,128)S(1)}, u32[]{:S(2)}, u32[]{:S(2)}) collective-permute-start(f32[3,72,128]{2,1,0:T(8,128)S(1)} %get-tuple-element.37), channel_id=1, source_target_pairs={{0,1},{1,2},{2,3},{3,4},{4,5},{5,6},{6,7},{7,8},{8,9},{9,10},{10,1... | collective-permute-start | bytes 331784 | tf_op jit(solution)/shard_map/ppermute | solution.py:807
  16.7 9.0 %collective-permute-start.3 = (f32[3,72,128]{2,1,0:T(8,128)S(1)}, f32[3,72,128]{2,1,0:T(8,128)S(1)}, u32[]{:S(2)}, u32[]{:S(2)}) collective-permute-start(f32[3,72,128]{2,1,0:T(8,128)S(1)} %get-tuple-element.38), channel_id=1, source_target_pairs={{1,0},{2,1},{3,2},{4,3},{5,4},{6,5},{7,6},{8,7},{9,8},{10,9},{11,1... | collective-permute-start | bytes 331784 | tf_op jit(solution)/shard_map/ppermute | solution.py:808
  21.5 12.9 %copy-start.7 = (f32[75,4]{0,1:T(4,128)S(1)}, f32[75,4]{0,1:T(4,128)}, u32[]{:S(2)}) copy-start(f32[75,4]{0,1:T(4,128)} %param.19) | copy-start | bytes 3604
  21.5 12.9 %copy-start.11 = (f32[74]{0:T(128)S(1)}, f32[74]{0:T(128)}, u32[]{:S(2)}) copy-start(f32[74]{0:T(128)} %k_ref.3) | copy-start | bytes 892
  25.7 27.9 %all-to-all-start = ((f32[128,1,2176]{2,1,0:T(1,128)}), f32[128,1,2176]{2,1,0:T(1,128)}, u32[]{:S(2)}, u32[]{:S(2)}) async-start(f32[128,1,2176]{2,1,0:T(1,128)} %bitcast.19), calls=%async_computation | async-start | bytes 2228224 | tf_op jit(solution)/shard_map/all_to_all | solution.py:813
  34.4 6.2 %copy-start.3 = (f32[75,64,128]{2,1,0:T(8,128)S(1)}, f32[75,64,128]{2,1,0:T(8,128)}, u32[]{:S(2)}) copy-start(f32[75,64,128]{2,1,0:T(8,128)} %x_ref.2) | copy-start | bytes 7372804
  56.2 24.1 %all-to-all-start.1 = ((f32[128,4,4,128]{3,2,1,0:T(4,128)}), f32[128,4,4,128]{3,2,1,0:T(4,128)S(1)}, u32[]{:S(2)}, u32[]{:S(2)}) async-start(f32[128,4,4,128]{3,2,1,0:T(4,128)} %bitcast.20), calls=%async_computation.1 | async-start | bytes 2097152 | tf_op jit(solution)/shard_map/all_to_all | solution.py:813
  62.8 5.6 %collective-permute-start.4 = (f32[5,2,128]{2,1,0:T(2,128)S(1)}, f32[5,2,128]{2,1,0:T(2,128)S(1)}, u32[]{:S(2)}, u32[]{:S(2)}) collective-permute-start(f32[5,2,128]{2,1,0:T(2,128)S(1)} %get-tuple-element.46), channel_id=1, source_target_pairs={{0,16},{16,32},{32,48},{48,64},{64,80},{80,96},{96,112},{1,17},{17... | collective-permute-start | bytes 15368 | tf_op jit(solution)/shard_map/ppermute | solution.py:798
  66.4 5.3 %collective-permute-start.5 = (f32[5,2,128]{2,1,0:T(2,128)S(1)}, f32[5,2,128]{2,1,0:T(2,128)S(1)}, u32[]{:S(2)}, u32[]{:S(2)}) collective-permute-start(f32[5,2,128]{2,1,0:T(2,128)S(1)} %get-tuple-element.47), channel_id=1, source_target_pairs={{16,0},{32,16},{48,32},{64,48},{80,64},{96,80},{112,96},{17,1},{33... | collective-permute-start | bytes 15368 | tf_op jit(solution)/shard_map/ppermute | solution.py:799
  71.7 1.7 %copy-start.5 = (f32[75,64,128]{2,1,0:T(8,128)S(1)}, f32[75,64,128]{2,1,0:T(8,128)}, u32[]{:S(2)}) copy-start(f32[75,64,128]{2,1,0:T(8,128)} %ocean_tangent.1.x_ref) | copy-start | bytes 7372804
  73.4 6.8 %copy-start.4 = (bf16[63,8192]{1,0:T(8,128)(2,1)S(1)}, bf16[63,8192]{1,0:T(8,128)(2,1)}, u32[]{:S(2)}) copy-start(bf16[63,8192]{1,0:T(8,128)(2,1)} %mix_ref.1) | copy-start | bytes 3096580

commit v3 on v2

--- a/solution.py
+++ b/solution.py
@@ -629,15 +629,18 @@
     )(k, ends, pen, x, mask, north, south, own, west, east)
 
 
-def answer_kernel(msg_ref, flux_ref, out_hbm, out_ref, sems):
+def answer_kernel(msg_hbm, flux_ref, out_hbm, label_ref, out_ref, sems):
     quarter = DEV // 4
+    fetch = pltpu.make_async_copy(msg_hbm.at[:, :, pl.ds((MSG - 1) * B, B)], label_ref, sems.at[4])
+    fetch.start()
     gh, gl = split2(flux_ref[...])
     table = jnp.concatenate([gh, gl], axis=0)
     want = lax.broadcasted_iota(jnp.int32, (quarter, B), 1) % OY + 1
     size = quarter * CAP * FLD
     copies = []
+    fetch.wait()
     for q in range(4):
-        labels = msg_ref[pl.ds(q * quarter * MSG + MSG - 1, quarter, stride=MSG), :].astype(jnp.int32)
+        labels = label_ref[pl.ds(q * quarter, quarter), 0, :].astype(jnp.int32)
         pick = jnp.concatenate(
             [(labels[:, c : c + 1] == want).astype(F32) for c in range(CAP)], axis=0
         ).astype(BF16)
@@ -656,10 +659,14 @@
 def answer(msg, flux):
     return pl.pallas_call(
         answer_kernel,
-        in_specs=[VMEM, VMEM],
+        in_specs=[ANY, VMEM],
         out_specs=ANY,
         out_shape=pltpu.HBM((DEV * CAP * FLD, B), F32),
-        scratch_shapes=[pltpu.VMEM((DEV * CAP * FLD, B), F32), pltpu.SemaphoreType.DMA((4,))],
+        scratch_shapes=[
+            pltpu.VMEM((DEV, 1, B), F32),
+            pltpu.VMEM((DEV * CAP * FLD, B), F32),
+            pltpu.SemaphoreType.DMA((5,)),
+        ],
         compiler_params=params(12),
         cost_estimate=cost(2.5),
         name="answer",
@@ -844,7 +851,8 @@
         lax.axis_size("tile"), target_device.T, target_row.T, pair, remap_weight
     )
     sent, west, east = lax.optimization_barrier((sent, west, east))
-    arrived = exchange(sent.reshape(DEV, 1, MSG * B)).reshape(DEV * MSG, B)
+    messages = exchange(sent.reshape(DEV, 1, MSG * B))
+    arrived = messages.reshape(DEV * MSG, B)
     ocean_backward, flux_adjoint = ocean_steps(
         True, ocean_mixing, ends, pen, ocean_adjoint, sea_mask, north, south, own, west, east
     )
@@ -852,7 +860,7 @@
         False, ocean_mixing, ends, pen, ocean_tangent, sea_mask, north, south, own, west, east
     )
     flux_adjoint, stepped = lax.optimization_barrier((flux_adjoint, stepped))
-    returned = exchange(answer(arrived, flux_adjoint).reshape(DEV, CAP, FLD, B))
+    returned = exchange(answer(messages, flux_adjoint).reshape(DEV, CAP, FLD, B))
     pen_1 = mix_levels(pen, ocean_mixing)
     pen_2 = mix_levels(pen_1, ocean_mixing)
     coefs = jnp.concatenate([pen_2, (2.0 * HRATE) * pen_1, (HRATE * HRATE) * pen], axis=0)

time: 87.6 us -> 87.6 us (level)
  no operation moved by 1% of the time
where the time goes in v3:
time: 87.6 us; the launch traced here: 87.2 us
  Pallas kernels  40.6 us (46%)
  starting transfers between devices  31.5 us (36%)
  waiting for transfers between devices  12 us (14%)
  local copies, waits for them, and re-layouts  1.75 us (2%)
  between operations  0.89 us (1%)
    all_to_all x2, starting transfers between devices, exchange(): lax.all_to_all(rows, ('face', 'tile'), split_axis=0, concat_axis=0, tiled...  13.2 us
    pallas_call x2, Pallas kernels, ocean_steps(): pl.pallas_call(functools.partial(ocean_kernel, adjoint), grid=(1,), in_sp...  12.5 us
    all_to_all x2, waiting for transfers between devices, exchange(): lax.all_to_all(rows, ('face', 'tile'), split_axis=0, concat_axis=0, tiled...  8.55 us
    ppermute x2, starting transfers between devices, swap_rows(): north = lax.ppermute(high_rows, 'face', south_going)  8.33 us
    pallas_call x1, Pallas kernels, atm_adjoint(): pl.pallas_call(atm_adjoint_kernel, in_specs=[SMEM, SMEM, VMEM, VMEM, ANY]...  6.9 us
    pallas_call x1, Pallas kernels, apply_flux(): pl.pallas_call(apply_flux_kernel, in_specs=[SMEM, SMEM] + [VMEM] * 6, out...  4.98 us
    ppermute x1, starting transfers between devices, swap_columns(): east = lax.ppermute(for_west, 'tile', west_going)  4.82 us
    pallas_call x1, Pallas kernels, surface_flux(): pl.pallas_call(surface_flux_kernel, in_specs=[SMEM, ANY, ANY], out_specs=...  4.42 us
  transfers between devices with their start and end apart: 8, of which 4 were waited for; matrix products, arithmetic and copies ran while one was open for 0% of the time, Pallas kernels for 32%

profile of v3, /device:TPU:1, one launch (start us, length us, event | category | flops | bytes accessed | tf_op | source)
XLA Modules:
  0.0 87.2 jit_solution(13612315773237601335)
XLA Ops:
  0.6 0.0 copy-start.9
  0.6 0.0 copy-start.1
  0.7 0.0 copy-start.2
  0.7 1.6 %edge_rows.1 = (f32[150,2,128]{2,1,0:T(2,128)S(1)}, f32[150,2,128]{2,1,0:T(2,128)S(1)}) custom-call(f32[75,64,128]{2,1,0:T(8,128)} %x_ref.2, f32[75,64,128]{2,1,0:T(8,128)} %x_ref.3, s32[64,128]{1,0:T(8,128)} %mask_ref.7), custom_call_target="tpu_custom_call" | custom-call | tf_op jit(solution)/shard_map/edge_rows/pallas_call | solution.py:379
  2.3 0.0 copy-start.6
  2.3 4.7 %collective-permute-start = (f32[150,2,128]{2,1,0:T(2,128)S(1)}, f32[150,2,128]{2,1,0:T(2,128)S(1)}, u32[]{:S(2)}, u32[]{:S(2)}) collective-permute-start(f32[150,2,128]{2,1,0:T(2,128)S(1)} %get-tuple-element.27), channel_id=1, source_target_pairs={{0,16},{16,32},{32,48},{48,64},{64,80},{80,96},{96,112},{1,17},{17... | collective-permute-start | bytes 460808 | tf_op jit(solution)/shard_map/ppermute | solution.py:805
  7.0 1.9 %collective-permute-start.1 = (f32[150,2,128]{2,1,0:T(2,128)S(1)}, f32[150,2,128]{2,1,0:T(2,128)S(1)}, u32[]{:S(2)}, u32[]{:S(2)}) collective-permute-start(f32[150,2,128]{2,1,0:T(2,128)S(1)} %get-tuple-element.28), channel_id=1, source_target_pairs={{16,0},{32,16},{48,32},{64,48},{80,64},{96,80},{112,96},{17,1},{33... | collective-permute-start | bytes 460808 | tf_op jit(solution)/shard_map/ppermute | solution.py:806
  8.9 0.0 copy-done.9
  8.9 0.0 copy-start
  9.0 4.4 %surface_flux.1.pair_ref = f32[512,128]{1,0:T(8,128)S(1)} custom-call(f32[4,64]{1,0:T(4,128)S(1)} %copy-done.9, f32[64,8192]{1,0:T(8,128)} %x_hbm.1, bf16[63,8192]{1,0:T(8,128)(2,1)} %mix_ref.1), custom_call_target="tpu_custom_call" | custom-call | tf_op jit(solution)/shard_map/surface_flux/pallas_call | solution.py:163
  13.4 0.0 copy-start.8
  13.4 0.0 copy-start.10
  13.4 0.0 collective-permute-done.north_ref
  13.4 0.1 collective-permute-done.1.south_ref
  13.5 0.0 copy-done.1
  13.5 0.0 copy-done.2
  13.5 0.0 copy-done.6
  13.5 1.9 %pack_columns.1 = (f32[2,3,72,128]{3,2,1,0:T(8,128)S(1)}, f32[3,72,128]{2,1,0:T(8,128)S(1)}, f32[3,72,128]{2,1,0:T(8,128)S(1)}) custom-call(f32[75,64,128]{2,1,0:T(8,128)S(1)} %copy-done.2, f32[75,64,128]{2,1,0:T(8,128)S(1)} %copy-done.1, s32[64,128]{1,0:T(8,128)S(1)} %copy-done.6, f32[150,2,128]{2,1,0:T(2,128)S(1)} %collective-permute-done.north_ref, ...), custom_call_target="tpu_custom_call" | custom-call | tf_op jit(solution)/shard_map/pack_columns/pallas_call | solution.py:434
  15.4 1.3 %collective-permute-start.2 = (f32[3,72,128]{2,1,0:T(8,128)S(1)}, f32[3,72,128]{2,1,0:T(8,128)S(1)}, u32[]{:S(2)}, u32[]{:S(2)}) collective-permute-start(f32[3,72,128]{2,1,0:T(8,128)S(1)} %get-tuple-element.37), channel_id=1, source_target_pairs={{0,1},{1,2},{2,3},{3,4},{4,5},{5,6},{6,7},{7,8},{8,9},{9,10},{10,1... | collective-permute-start | bytes 331784 | tf_op jit(solution)/shard_map/ppermute | solution.py:814
  16.7 4.8 %collective-permute-start.3 = (f32[3,72,128]{2,1,0:T(8,128)S(1)}, f32[3,72,128]{2,1,0:T(8,128)S(1)}, u32[]{:S(2)}, u32[]{:S(2)}) collective-permute-start(f32[3,72,128]{2,1,0:T(8,128)S(1)} %get-tuple-element.38), channel_id=1, source_target_pairs={{1,0},{2,1},{3,2},{4,3},{5,4},{6,5},{7,6},{8,7},{9,8},{10,9},{11,1... | collective-permute-start | bytes 331784 | tf_op jit(solution)/shard_map/ppermute | solution.py:815
  21.5 0.0 copy-done
  21.5 0.0 copy-done.8
  21.5 0.0 copy-done.10
  21.5 0.0 copy-start.11
  21.6 4.2 %remap.1 = (f32[2176,128]{1,0:T(8,128)}, s32[256]{0:T(256)S(1)}) custom-call(s32[4,64]{1,0:T(4,128)S(1)} %bitcast.16, s32[4,64]{1,0:T(4,128)S(1)} %bitcast.17, s32[4,64]{1,0:T(4,128)S(1)} %bitcast.18, f32[512,128]{1,0:T(8,128)S(1)} %surface_flux.1.pair_ref, bf16[256,128,128]{2,1,0:T(8,128)(2,1)S(1)} %copy-done), custom_call_target="tpu_custom_call" | custom-call | tf_op jit(solution)/shard_map/remap/pallas_call | solution.py:264
  25.7 0.0 collective-permute-done.2.west_ref
  25.7 0.0 collective-permute-done.3.east_ref
  25.7 8.6 %all-to-all-start = ((f32[128,1,2176]{2,1,0:T(1,128)}), f32[128,1,2176]{2,1,0:T(1,128)}, u32[]{:S(2)}, u32[]{:S(2)}) async-start(f32[128,1,2176]{2,1,0:T(1,128)} %bitcast.19), calls=%async_computation | async-start | bytes 2228224 | tf_op jit(solution)/shard_map/all_to_all | solution.py:820
  34.3 0.1 add_convert_fusion.ends_ref
  34.4 0.0 copy-done.11
  34.4 6.2 %ocean_tangent.1.x_ref = f32[75,64,128]{2,1,0:T(8,128)} custom-call(f32[74]{0:T(128)S(1)} %copy-done.11, s32[2]{0:T(128)S(1)} %add_convert_fusion.ends_ref, f32[4,75]{1,0:T(4,128)S(1)} %bitcast.13, f32[75,64,128]{2,1,0:T(8,128)S(1)} %copy-done.1, s32[64,128]{1,0:T(8,128)S(1)} %copy-done.6, f32[150,2,128]{2,1,0:T(2,128)S(1)} %collective-permute-done.north_ref, ...), custom_call_target="tpu_custom_call" | custom-call | flops 1800000000 | bytes 5400000 | tf_op jit(solution)/shard_map/ocean_tangent/pallas_call | solution.py:602
  40.7 6.3 %ocean_adjoint.1 = (f32[75,64,128]{2,1,0:T(8,128)}, f32[64,512]{1,0:T(8,128)S(1)}) custom-call(f32[74]{0:T(128)S(1)} %copy-done.11, s32[2]{0:T(128)S(1)} %add_convert_fusion.ends_ref, f32[4,75]{1,0:T(4,128)S(1)} %bitcast.14, f32[75,64,128]{2,1,0:T(8,128)S(1)} %copy-done.3, s32[64,128]{1,0:T(8,128)S(1)} %copy-done.6, ...), custom_call_target="tpu_custom_call" | custom-call | flops 1800000000 | bytes 5400000 | tf_op jit(solution)/shard_map/ocean_adjoint/pallas_call | solution.py:602
  46.9 6.7 %all-to-all-done.msg_hbm = f32[128,1,2176]{2,1,0:T(1,128)} async-done(((f32[128,1,2176]{2,1,0:T(1,128)}), f32[128,1,2176]{2,1,0:T(1,128)}, u32[]{:S(2)}, u32[]{:S(2)}) %all-to-all-start) | async-done | bytes 1114144 | tf_op jit(solution)/shard_map/all_to_all | solution.py:820
  53.7 2.5 %answer.1 = f32[2048,128]{1,0:T(8,128)} custom-call(f32[128,1,2176]{2,1,0:T(1,128)} %all-to-all-done.msg_hbm, f32[64,512]{1,0:T(8,128)S(1)} %get-tuple-element.50.flux_ref), custom_call_target="tpu_custom_call" | custom-call | flops 750000000 | bytes 2250000 | tf_op jit(solution)/shard_map/answer/pallas_call | solution.py:660
  56.2 4.6 %all-to-all-start.1 = ((f32[128,4,4,128]{3,2,1,0:T(4,128)}), f32[128,4,4,128]{3,2,1,0:T(4,128)S(1)}, u32[]{:S(2)}, u32[]{:S(2)}) async-start(f32[128,4,4,128]{3,2,1,0:T(4,128)} %bitcast.20), calls=%async_computation.1 | async-start | bytes 2097152 | tf_op jit(solution)/shard_map/all_to_all | solution.py:820
  60.8 0.1 subtract_multiply_fusion.1
  60.9 0.1 broadcast_multiply_fusion.1
  61.0 0.1 subtract_multiply_fusion
  61.1 0.1 pad_subtract_fusion
  61.1 1.7 %collect.1 = (f32[4,64,128]{2,1,0:T(8,128)S(1)}, f32[64,128]{1,0:T(8,128)S(1)}, f32[5,2,128]{2,1,0:T(2,128)S(1)}, f32[5,2,128]{2,1,0:T(2,128)S(1)}) custom-call(f32[2176,128]{1,0:T(8,128)} %bitcast.6.msg_ref), custom_call_target="tpu_custom_call" | custom-call | flops 480000000 | bytes 1440000 | tf_op jit(solution)/shard_map/collect/pallas_call | solution.py:715
  62.8 3.6 %collective-permute-start.4 = (f32[5,2,128]{2,1,0:T(2,128)S(1)}, f32[5,2,128]{2,1,0:T(2,128)S(1)}, u32[]{:S(2)}, u32[]{:S(2)}) collective-permute-start(f32[5,2,128]{2,1,0:T(2,128)S(1)} %get-tuple-element.46), channel_id=1, source_target_pairs={{0,16},{16,32},{32,48},{48,64},{64,80},{80,96},{96,112},{1,17},{17... | collective-permute-start | bytes 15368 | tf_op jit(solution)/shard_map/ppermute | solution.py:805
  66.4 1.9 %collective-permute-start.5 = (f32[5,2,128]{2,1,0:T(2,128)S(1)}, f32[5,2,128]{2,1,0:T(2,128)S(1)}, u32[]{:S(2)}, u32[]{:S(2)}) collective-permute-start(f32[5,2,128]{2,1,0:T(2,128)S(1)} %get-tuple-element.47), channel_id=1, source_target_pairs={{16,0},{32,16},{48,32},{64,48},{80,64},{96,80},{112,96},{17,1},{33... | collective-permute-start | bytes 15368 | tf_op jit(solution)/shard_map/ppermute | solution.py:806
  68.4 0.0 collective-permute-done.4.north_ref
  68.4 3.3 %collective-permute-done.5.south_ref = f32[5,2,128]{2,1,0:T(2,128)S(1)} collective-permute-done((f32[5,2,128]{2,1,0:T(2,128)S(1)}, f32[5,2,128]{2,1,0:T(2,128)S(1)}, u32[]{:S(2)}, u32[]{:S(2)}) %collective-permute-start.5) | collective-permute-done | bytes 5152 | tf_op jit(solution)/shard_map/ppermute | solution.py:806
  71.7 1.7 %copy-done.5 = f32[75,64,128]{2,1,0:T(8,128)S(1)} copy-done((f32[75,64,128]{2,1,0:T(8,128)S(1)}, f32[75,64,128]{2,1,0:T(8,128)}, u32[]{:S(2)}) %copy-start.5) | copy-done | bytes 2457624
  73.4 5.0 %apply_flux.1 = f32[75,64,128]{2,1,0:T(8,128)} custom-call(f32[12,75]{1,0:T(8,128)S(1)} %pad_maximum_fusion.coef_ref, s32[2]{0:T(128)S(1)} %add_convert_fusion.ends_ref, f32[75,64,128]{2,1,0:T(8,128)S(1)} %copy-done.5, s32[64,128]{1,0:T(8,128)S(1)} %copy-done.6, f32[4,64,128]{2,1,0:T(8,128)S(1)} %get-tuple-element.44.flux_ref, ...), custom_call_target="tpu_custom_call" | custom-call | tf_op jit(solution)/shard_map/apply_flux/pallas_call | solution.py:786
  78.4 1.8 %all-to-all-done.1 = f32[128,4,4,128]{3,2,1,0:T(4,128)S(1)} async-done(((f32[128,4,4,128]{3,2,1,0:T(4,128)}), f32[128,4,4,128]{3,2,1,0:T(4,128)S(1)}, u32[]{:S(2)}, u32[]{:S(2)}) %all-to-all-start.1) | async-done | bytes 1048608 | tf_op jit(solution)/shard_map/all_to_all | solution.py:820
  80.3 6.9 %atm_adjoint.1 = f32[64,8192]{1,0:T(8,128)} custom-call(s32[256]{0:T(256)S(1)} %get-tuple-element.49.slot_ref, f32[4,64]{1,0:T(4,128)S(1)} %copy-done.9, f32[512,4,128]{2,1,0:T(4,128)S(1)} %bitcast.12, bf16[63,8192]{1,0:T(8,128)(2,1)S(1)} %copy-done.4, bf16[256,128,128]{2,1,0:T(8,128)(2,1)} %w_hbm.1), custom_call_target="tpu_custom_call" | custom-call | tf_op jit(solution)/shard_map/atm_adjoint/pallas_call | solution.py:341
  (8 shorter events, 0.0 us)
Async XLA Ops:
  0.6 8.3 %copy-start.9 = (f32[4,64]{1,0:T(4,128)S(1)}, f32[4,64]{1,0:T(4,128)}, u32[]{:S(2)}) copy-start(f32[4,64]{1,0:T(4,128)} %coef_ref.3) | copy-start | bytes 3076
  0.6 12.9 %copy-start.1 = (f32[75,64,128]{2,1,0:T(8,128)S(1)}, f32[75,64,128]{2,1,0:T(8,128)}, u32[]{:S(2)}) copy-start(f32[75,64,128]{2,1,0:T(8,128)} %x_ref.3) | copy-start | bytes 7372804
  0.7 12.9 %copy-start.2 = (f32[75,64,128]{2,1,0:T(8,128)S(1)}, f32[75,64,128]{2,1,0:T(8,128)}, u32[]{:S(2)}) copy-start(f32[75,64,128]{2,1,0:T(8,128)} %x_ref.2) | copy-start | bytes 7372804
  2.3 11.3 %copy-start.6 = (s32[64,128]{1,0:T(8,128)S(1)}, s32[64,128]{1,0:T(8,128)}, u32[]{:S(2)}) copy-start(s32[64,128]{1,0:T(8,128)} %mask_ref.7) | copy-start | bytes 98308
  2.3 11.1 %collective-permute-start = (f32[150,2,128]{2,1,0:T(2,128)S(1)}, f32[150,2,128]{2,1,0:T(2,128)S(1)}, u32[]{:S(2)}, u32[]{:S(2)}) collective-permute-start(f32[150,2,128]{2,1,0:T(2,128)S(1)} %get-tuple-element.27), channel_id=1, source_target_pairs={{0,16},{16,32},{32,48},{48,64},{64,80},{80,96},{96,112},{1,17},{17... | collective-permute-start | bytes 460808 | tf_op jit(solution)/shard_map/ppermute | solution.py:805
  7.0 6.5 %collective-permute-start.1 = (f32[150,2,128]{2,1,0:T(2,128)S(1)}, f32[150,2,128]{2,1,0:T(2,128)S(1)}, u32[]{:S(2)}, u32[]{:S(2)}) collective-permute-start(f32[150,2,128]{2,1,0:T(2,128)S(1)} %get-tuple-element.28), channel_id=1, source_target_pairs={{16,0},{32,16},{48,32},{64,48},{80,64},{96,80},{112,96},{17,1},{33... | collective-permute-start | bytes 460808 | tf_op jit(solution)/shard_map/ppermute | solution.py:806
  8.9 12.6 %copy-start = (bf16[256,128,128]{2,1,0:T(8,128)(2,1)S(1)}, bf16[256,128,128]{2,1,0:T(8,128)(2,1)}, u32[]{:S(2)}) copy-start(bf16[256,128,128]{2,1,0:T(8,128)(2,1)} %w_hbm.1) | copy-start | bytes 25165828
  13.4 8.2 %copy-start.8 = (s32[64,4]{0,1:T(4,128)S(1)}, s32[64,4]{0,1:T(4,128)}, u32[]{:S(2)}) copy-start(s32[64,4]{0,1:T(4,128)} %param.15) | copy-start | bytes 3076
  13.4 8.1 %copy-start.10 = (s32[64,4]{0,1:T(4,128)S(1)}, s32[64,4]{0,1:T(4,128)}, u32[]{:S(2)}) copy-start(s32[64,4]{0,1:T(4,128)} %param.16) | copy-start | bytes 3076
  15.4 10.3 %collective-permute-start.2 = (f32[3,72,128]{2,1,0:T(8,128)S(1)}, f32[3,72,128]{2,1,0:T(8,128)S(1)}, u32[]{:S(2)}, u32[]{:S(2)}) collective-permute-start(f32[3,72,128]{2,1,0:T(8,128)S(1)} %get-tuple-element.37), channel_id=1, source_target_pairs={{0,1},{1,2},{2,3},{3,4},{4,5},{5,6},{6,7},{7,8},{8,9},{9,10},{10,1... | collective-permute-start | bytes 331784 | tf_op jit(solution)/shard_map/ppermute | solution.py:814
  16.7 9.0 %collective-permute-start.3 = (f32[3,72,128]{2,1,0:T(8,128)S(1)}, f32[3,72,128]{2,1,0:T(8,128)S(1)}, u32[]{:S(2)}, u32[]{:S(2)}) collective-permute-start(f32[3,72,128]{2,1,0:T(8,128)S(1)} %get-tuple-element.38), channel_id=1, source_target_pairs={{1,0},{2,1},{3,2},{4,3},{5,4},{6,5},{7,6},{8,7},{9,8},{10,9},{11,1... | collective-permute-start | bytes 331784 | tf_op jit(solution)/shard_map/ppermute | solution.py:815
  21.5 12.9 %copy-start.7 = (f32[75,4]{0,1:T(4,128)S(1)}, f32[75,4]{0,1:T(4,128)}, u32[]{:S(2)}) copy-start(f32[75,4]{0,1:T(4,128)} %param.19) | copy-start | bytes 3604
  21.5 12.9 %copy-start.11 = (f32[74]{0:T(128)S(1)}, f32[74]{0:T(128)}, u32[]{:S(2)}) copy-start(f32[74]{0:T(128)} %k_ref.3) | copy-start | bytes 892
  25.7 27.9 %all-to-all-start = ((f32[128,1,2176]{2,1,0:T(1,128)}), f32[128,1,2176]{2,1,0:T(1,128)}, u32[]{:S(2)}, u32[]{:S(2)}) async-start(f32[128,1,2176]{2,1,0:T(1,128)} %bitcast.19), calls=%async_computation | async-start | bytes 2228224 | tf_op jit(solution)/shard_map/all_to_all | solution.py:820
  34.4 6.2 %copy-start.3 = (f32[75,64,128]{2,1,0:T(8,128)S(1)}, f32[75,64,128]{2,1,0:T(8,128)}, u32[]{:S(2)}) copy-start(f32[75,64,128]{2,1,0:T(8,128)} %x_ref.2) | copy-start | bytes 7372804
  56.2 24.1 %all-to-all-start.1 = ((f32[128,4,4,128]{3,2,1,0:T(4,128)}), f32[128,4,4,128]{3,2,1,0:T(4,128)S(1)}, u32[]{:S(2)}, u32[]{:S(2)}) async-start(f32[128,4,4,128]{3,2,1,0:T(4,128)} %bitcast.20), calls=%async_computation.1 | async-start | bytes 2097152 | tf_op jit(solution)/shard_map/all_to_all | solution.py:820
  62.8 5.6 %collective-permute-start.4 = (f32[5,2,128]{2,1,0:T(2,128)S(1)}, f32[5,2,128]{2,1,0:T(2,128)S(1)}, u32[]{:S(2)}, u32[]{:S(2)}) collective-permute-start(f32[5,2,128]{2,1,0:T(2,128)S(1)} %get-tuple-element.46), channel_id=1, source_target_pairs={{0,16},{16,32},{32,48},{48,64},{64,80},{80,96},{96,112},{1,17},{17... | collective-permute-start | bytes 15368 | tf_op jit(solution)/shard_map/ppermute | solution.py:805
  66.4 5.3 %collective-permute-start.5 = (f32[5,2,128]{2,1,0:T(2,128)S(1)}, f32[5,2,128]{2,1,0:T(2,128)S(1)}, u32[]{:S(2)}, u32[]{:S(2)}) collective-permute-start(f32[5,2,128]{2,1,0:T(2,128)S(1)} %get-tuple-element.47), channel_id=1, source_target_pairs={{16,0},{32,16},{48,32},{64,48},{80,64},{96,80},{112,96},{17,1},{33... | collective-permute-start | bytes 15368 | tf_op jit(solution)/shard_map/ppermute | solution.py:806
  71.7 1.7 %copy-start.5 = (f32[75,64,128]{2,1,0:T(8,128)S(1)}, f32[75,64,128]{2,1,0:T(8,128)}, u32[]{:S(2)}) copy-start(f32[75,64,128]{2,1,0:T(8,128)} %ocean_tangent.1.x_ref) | copy-start | bytes 7372804
  73.4 6.8 %copy-start.4 = (bf16[63,8192]{1,0:T(8,128)(2,1)S(1)}, bf16[63,8192]{1,0:T(8,128)(2,1)}, u32[]{:S(2)}) copy-start(bf16[63,8192]{1,0:T(8,128)(2,1)} %mix_ref.1) | copy-start | bytes 3096580
